TPU v7x, 32 devices: a whole 2x2x4 slice. The times are simulated.
32 devices in a mesh: row: 4 (over y, x), col: 8 (over z, core).
Axes of the slice: x: 2, y: 2, z: 4, core: 2. Of those that a mesh axis runs over, the one named last changes fastest.
Arguments:
- trailing: bfloat16 [4096, 8192], P('row', 'col'), may hold values from -6 to 6
- raw_l: bfloat16 [4, 16, 1024, 1024], P('row', None, 'col'), may hold values from -1.1953125 to 1.1953125
- raw_u: bfloat16 [16, 8, 1024, 1024], P(None, 'col', 'row'), may hold values from -1.1953125 to 1.1953125
- sketch: bfloat16 [4, 8, 1024, 192], P('row', 'col'), may hold values from -0.1875 to 0.1875
- helper_l: int32 [4, 16], P('row'), may hold values from 0 to 7, as said below
- helper_u: int32 [16, 8], P(None, 'col'), may hold values from 0 to 3, as said below
- ranks_l: int32 [4, 16], P('row'), may hold values from 64 to 192, as said below
- ranks_u: int32 [16, 8], P(None, 'col'), may hold values from 64 to 192, as said below
Outputs:
- updated: float32 [4096, 8192], P('row', 'col')
Inputs may be any that keep to these rules, and one draw needn't show every extreme that they name: `helper_l`: in every grid row no value occurs more than 4 times, and some value occurs exactly 4 times. `helper_u`: in every grid column no value occurs more than 8 times, and some value occurs exactly 8 times. `ranks_l`: some tile has rank 64 and some tile rank 192. `ranks_u`: some tile has rank 64 and some tile rank 192.
All inputs are finite; a program needn't handle non-finite values.
Results may differ from a plain program's by a relative error of at most 0.0068.
Values may be sent and summed in bfloat16 or wider, within the bound.
No kernel may reach another device: no remote copies, remote signals or barrier semaphores. Data moves between devices by JAX's collectives and lax.ppermute only.
A program may use at most 192 MiB of HBM per device.

v0:
```python
import jax
import jax.numpy as jnp
from jax import lax
from jax.sharding import PartitionSpec as P


def compress_tile(panel_tile, tile_rank, sketch_cols):
    keep_cols = jnp.arange(sketch_cols.shape[1]) < tile_rank
    masked = jnp.where(keep_cols[None, :], sketch_cols, jnp.zeros_like(sketch_cols))
    sketched = jnp.dot(panel_tile, masked, preferred_element_type=jnp.float32)
    padding = jnp.where(keep_cols, 0.0, 1.0).astype(jnp.float32)
    gram = jnp.dot(sketched.T, sketched, precision=lax.Precision.HIGHEST) + jnp.diag(padding)
    lower_factor = jnp.linalg.cholesky(gram)
    basis = jax.scipy.linalg.solve_triangular(lower_factor, sketched.T, lower=True).T.astype(
        jnp.bfloat16
    )
    coeffs = lax.dot_general(
        panel_tile, basis, (((0,), (0,)), ((), ())), preferred_element_type=jnp.float32
    ).astype(jnp.bfloat16)
    return jnp.concatenate([basis, coeffs], axis=1)


def slot_numbers(helpers):
    total = helpers.shape[0]
    same_helper = helpers[:, None] == helpers[None, :]
    earlier = jnp.arange(total)[None, :] < jnp.arange(total)[:, None]
    return jnp.sum(jnp.logical_and(same_helper, earlier).astype(jnp.int32), axis=1)


def pack_slabs(slabs, helpers, slots, owners, capacity):
    target = slots * owners + helpers
    table = (jnp.arange(capacity * owners)[:, None] == target[None, :]).astype(jnp.bfloat16)
    packed = jnp.einsum("sk,kab->sab", table, slabs, preferred_element_type=jnp.float32).astype(
        jnp.bfloat16
    )
    return packed.reshape(capacity, owners * slabs.shape[1], slabs.shape[2])


def slot_ranks(ranks, helpers, slots, myself, capacity):
    chosen = jnp.logical_and(
        helpers[None, :] == myself, slots[None, :] == jnp.arange(capacity)[:, None]
    )
    return jnp.sum(jnp.where(chosen, ranks[None, :], 0), axis=1)


def pick_mine(returned, helpers, slots, capacity):
    target = helpers * capacity + slots
    table = (target[:, None] == jnp.arange(returned.shape[0])[None, :]).astype(jnp.bfloat16)
    return jnp.einsum("kn,nab->kab", table, returned, preferred_element_type=jnp.float32).astype(
        jnp.bfloat16
    )


def local(trailing, raw_l, raw_u, sketch, helper_l, helper_u, ranks_l, ranks_u):
    depth = raw_l.shape[1]
    width_r = sketch.shape[3]
    own_sketch = sketch[0, 0]
    compress_all = jax.vmap(compress_tile, in_axes=(0, 0, None))
    col_count = lax.axis_size("col")
    row_count = lax.axis_size("row")
    cap_row = 2 * depth // col_count
    cap_col = 2 * depth // row_count
    helpers_row = helper_l[0]
    slots_row = slot_numbers(helpers_row)
    sent_row = pack_slabs(raw_l[0], helpers_row, slots_row, col_count, cap_row)
    tiles_row = lax.all_to_all(sent_row, "col", split_axis=1, concat_axis=1, tiled=True)
    made_row = compress_all(
        tiles_row,
        slot_ranks(ranks_l[0], helpers_row, slots_row, lax.axis_index("col"), cap_row),
        own_sketch,
    )
    helpers_col = helper_u[:, 0]
    slots_col = slot_numbers(helpers_col)
    sent_col = pack_slabs(raw_u[:, 0], helpers_col, slots_col, row_count, cap_col)
    tiles_col = lax.all_to_all(sent_col, "row", split_axis=1, concat_axis=1, tiled=True)
    made_col = compress_all(
        tiles_col,
        slot_ranks(ranks_u[:, 0], helpers_col, slots_col, lax.axis_index("row"), cap_col),
        own_sketch,
    )
    back_row = lax.all_to_all(made_row, "col", split_axis=1, concat_axis=0, tiled=True)
    full_row = lax.all_gather(
        pick_mine(back_row, helpers_row, slots_row, cap_row), "col", axis=1, tiled=True
    )
    back_col = lax.all_to_all(made_col, "row", split_axis=1, concat_axis=0, tiled=True)
    full_col = lax.all_gather(
        pick_mine(back_col, helpers_col, slots_col, cap_col), "row", axis=1, tiled=True
    )
    basis_row = full_row[:, :, :width_r]
    coeff_row = full_row[:, :, width_r:]
    basis_col = full_col[:, :, :width_r]
    coeff_col = full_col[:, :, width_r:]
    middle = jnp.einsum(
        "kbr,kbs->krs", coeff_row, basis_col, preferred_element_type=jnp.float32
    ).astype(jnp.bfloat16)
    left = jnp.einsum("kbr,krs->kbs", basis_row, middle, preferred_element_type=jnp.float32).astype(
        jnp.bfloat16
    )
    update = jnp.einsum("kbs,kcs->bc", left, coeff_col, preferred_element_type=jnp.float32)
    return trailing.astype(jnp.float32) - update


def solution(mesh):
    placed = (
        P("row", "col"),
        P("row", None, "col", None),
        P(None, "col", "row", None),
        P("row", "col", None, None),
        P("row", None),
        P(None, "col"),
        P("row", None),
        P(None, "col"),
    )
    return jax.shard_map(
        local, mesh=mesh, in_specs=placed, out_specs=P("row", "col"), check_vma=False
    )
```

profile of v0, /device:TPU:0, one launch (start us, length us, event | category | flops | bytes accessed | tf_op | source)
XLA Modules:
  0.0 1509.1 jit_solution(15059634355706905019)
XLA Ops:
  8.1 12.6 convolution_convert_fusion
  20.7 15.4 %copy.85 = bf16[32,256,1024]{2,1,0:T(8,128)(2,1)S(1)} copy(bf16[32,256,1024]{2,0,1:T(8,128)(2,1)} %convolution_convert_fusion) | data formatting | bytes 33554432 | tf_op jit(solution)/shard_map/convert_element_type | solution.py:33
  36.1 31.0 %copy.86 = bf16[8,1024,1024]{2,0,1:T(8,128)(2,1)} copy(bf16[8,1024,1024]{2,1,0:T(8,128)(2,1)S(1)} %bitcast.127) | data formatting | bytes 33554432 | tf_op jit(solution)/shard_map/reshape | solution.py:36
  74.6 183.3 %all-to-all-done.2 = bf16[8,1024,1024]{2,0,1:T(8,128)(2,1)} async-done(((bf16[8,1024,1024]{2,0,1:T(8,128)(2,1)}), bf16[8,1024,1024]{2,0,1:T(8,128)(2,1)}, u32[]{:S(2)}, u32[]{:S(2)}) %all-to-all-start.2) | async-done | bytes 16777248 | tf_op jit(solution)/shard_map/all_to_all | solution.py:75
  257.9 30.6 %fusion.2 = f32[8,1024,192]{1,2,0:T(8,128)S(1)} fusion(bf16[8,1024,1024]{2,0,1:T(8,128)(2,1)} %all-to-all-done.2, pred[8,192]{1,0:T(8,128)(4,1)S(1)} %iota_compare_fusion.9, bf16[1024,192]{0,1:T(8,128)(2,1)S(1)} %bitcast.140), kind=kOutput, calls=%fused_computation.2 | convolution fusion | flops 3222798336 | bytes 23463424 | tf_op jit(solution)/shard_map/vmap()/dot_general | solution.py:10
  301.8 93.8 %custom-call.38 = f32[8,128,128]{2,1,0:T(8,128)S(1)} custom-call(f32[8,128,128]{2,1,0:T(8,128)S(1)} %cholesky.246), custom_call_target="Cholesky" | custom-call | tf_op jit(solution)/shard_map/vmap(jit(cholesky))/cholesky | solution.py:13
  395.8 78.8 %custom-call.39 = f32[8,1,128,128]{2,3,1,0:T(8,128)S(1)} custom-call(f32[8,1,128,128]{3,2,1,0:T(8,128)S(1)} %get-tuple-element.50), custom_call_target="InvertDiagBlocksLowerTriangular" | custom-call | tf_op jit(solution)/shard_map/vmap(jit(cholesky))/cholesky | solution.py:13
  477.7 46.9 %custom-call.40 = f32[8,64,64]{2,1,0:T(8,128)S(1)} custom-call(f32[8,64,64]{2,1,0:T(8,128)S(1)} %convolution_subtract_fusion.1), custom_call_target="Cholesky" | custom-call | tf_op jit(solution)/shard_map/vmap(jit(cholesky))/cholesky | solution.py:13
  525.5 157.9 %custom-call.41 = f32[8,2,128,128]{2,3,1,0:T(8,128)} custom-call(f32[8,2,128,128]{3,2,1,0:T(8,128)S(1)} %pad_maximum_fusion.5), custom_call_target="InvertDiagBlocksLowerTriangular" | custom-call | tf_op jit(solution)/shard_map/vmap(jit(_solve_triangular))/triangular_solve | solution.py:14
  698.2 27.7 %fusion.32 = bf16[8,1024,192]{1,2,0:T(8,128)(2,1)} fusion(bf16[8,1024,1024]{2,0,1:T(8,128)(2,1)} %all-to-all-done.2, bf16[8,64,1024]{2,1,0:T(8,128)(2,1)} %copy-done.3, bf16[8,128,1024]{2,1,0:T(8,128)(2,1)} %copy-done.1), kind=kOutput, calls=%fused_computation.33 | convolution fusion | flops 3229089792 | bytes 23068672 | tf_op jit(solution)/shard_map/vmap()/dot_general | solution.py:17
  755.0 11.3 copy.71
  766.4 12.2 copy.72
  778.5 37.1 %all-to-all-done.3 = bf16[8,1024,384]{2,0,1:T(8,128)(2,1)} async-done(((bf16[8,1024,384]{2,0,1:T(8,128)(2,1)}), bf16[8,1024,384]{2,0,1:T(8,128)(2,1)}, u32[]{:S(2)}, u32[]{:S(2)}) %all-to-all-start.3) | async-done | bytes 6291488 | tf_op jit(solution)/shard_map/all_to_all | solution.py:85
  827.4 177.2 %all-to-all-done = bf16[4,1024,1024]{2,0,1:T(4,128)(2,1)} async-done(((bf16[4,1024,1024]{2,0,1:T(4,128)(2,1)}), bf16[4,1024,1024]{2,0,1:T(4,128)(2,1)}, u32[]{:S(2)}, u32[]{:S(2)}) %all-to-all-start) | async-done | bytes 8388640 | tf_op jit(solution)/shard_map/all_to_all | solution.py:66
  1023.0 48.1 %custom-call.34 = f32[4,128,128]{2,1,0:T(8,128)S(1)} custom-call(f32[4,128,128]{2,1,0:T(8,128)} %cholesky.243), custom_call_target="Cholesky" | custom-call | tf_op jit(solution)/shard_map/vmap(jit(cholesky))/cholesky | solution.py:13
  1073.3 40.1 %custom-call.35 = f32[4,1,128,128]{2,3,1,0:T(8,128)S(1)} custom-call(f32[4,1,128,128]{3,2,1,0:T(8,128)} %get-tuple-element.52), custom_call_target="InvertDiagBlocksLowerTriangular" | custom-call | tf_op jit(solution)/shard_map/vmap(jit(cholesky))/cholesky | solution.py:13
  1116.6 23.5 %custom-call.36 = f32[4,64,64]{2,1,0:T(8,128)S(1)} custom-call(f32[4,64,64]{2,1,0:T(8,128)S(1)} %convolution_subtract_fusion.2), custom_call_target="Cholesky" | custom-call | tf_op jit(solution)/shard_map/vmap(jit(cholesky))/cholesky | solution.py:13
  1145.5 80.2 %custom-call.37 = f32[4,2,128,128]{2,3,1,0:T(8,128)} custom-call(f32[4,2,128,128]{3,2,1,0:T(8,128)} %pad_maximum_fusion.7), custom_call_target="InvertDiagBlocksLowerTriangular" | custom-call | tf_op jit(solution)/shard_map/vmap(jit(_solve_triangular))/triangular_solve | solution.py:14
  1249.6 71.4 %all-to-all-done.1 = bf16[4,1024,384]{2,0,1:T(4,128)(2,1)S(1)} async-done(((bf16[4,1024,384]{2,0,1:T(4,128)(2,1)}), bf16[4,1024,384]{2,0,1:T(4,128)(2,1)S(1)}, u32[]{:S(2)}, u32[]{:S(2)}) %all-to-all-start.1) | async-done | bytes 3145760 | tf_op jit(solution)/shard_map/all_to_all | solution.py:81
  1330.2 14.1 fusion.99
  1344.3 100.7 %all-gather.3.cloned.1.call-done = bf16[16,1024,384]{2,0,1:T(8,128)(2,1)} async-done(((bf16[16,128,384]{2,0,1:T(8,128)(2,1)}), bf16[16,1024,384]{2,0,1:T(8,128)(2,1)}) %all-gather.3.cloned.1.call-update) | async-done | bytes 12582928 | tf_op jit(solution)/shard_map/all_gather | solution.py:82
  1445.0 12.9 fusion.98
  1458.0 16.6 %fusion.48 = bf16[16,192,192]{2,1,0:T(8,128)(2,1)} fusion(bf16[16,1024,192]{2,0,1:T(8,128)(2,1)} %get-tuple-element.47, bf16[16,1024,192]{2,0,1:T(8,128)(2,1)} %get-tuple-element.46), kind=kOutput, calls=%fused_computation.41 | convolution fusion | flops 1208549376 | bytes 13762560 | tf_op jit(solution)/shard_map/kbr,kbs->krs/dot_general | solution.py:93
  1474.5 27.3 %bitcast_subtract_fusion = f32[1024,1024]{1,0:T(8,128)} fusion(bf16[1024,1024]{1,0:T(8,128)(2,1)S(1)} %copy-done.11, bf16[16,1024,192]{2,0,1:T(8,128)(2,1)} %get-tuple-element.48, bf16[16,192,192]{2,1,0:T(8,128)(2,1)} %fusion.48, bf16[16,1024,192]{2,0,1:T(8,128)(2,1)} %get-tuple-element.45), kind=kOutput, calls=%fused_computation.25 | convolution fusion | flops 7655653376 | bytes 20054016 | tf_op jit(solution)/shard_map/kbs,kcs->bc/dot_general | solution.py:99
  (116 shorter events, 144.3 us)
Async XLA Ops:
  67.1 7.1 copy-start.13
  67.1 7.2 copy-start.7
  67.1 190.9 %copy-start.12 = (bf16[1,1,1024,192]{2,3,1,0:T(8,128)(2,1)S(1)}, bf16[1,1,1024,192]{2,3,1,0:T(8,128)(2,1)}, u32[]{:S(2)}) copy-start(bf16[1,1,1024,192]{2,3,1,0:T(8,128)(2,1)} %param.11) | copy-start | bytes 1179652
  67.1 190.9 %all-to-all-start.2 = ((bf16[8,1024,1024]{2,0,1:T(8,128)(2,1)}), bf16[8,1024,1024]{2,0,1:T(8,128)(2,1)}, u32[]{:S(2)}, u32[]{:S(2)}) async-start(bf16[8,1024,1024]{2,0,1:T(8,128)(2,1)} %copy.86), calls=%async_computation.2 | async-start | bytes 33554432 | tf_op jit(solution)/shard_map/all_to_all | solution.py:75
  74.4 450.3 %copy-start.6 = (pred[64,64]{1,0:T(8,128)(4,1)}, pred[64,64]{1,0:T(8,128)(4,1)S(1)}, u32[]{:S(2)}) copy-start(pred[64,64]{1,0:T(8,128)(4,1)S(1)} %iota_compare_fusion.8) | copy-start | bytes 12292
  288.5 2.7 copy-start
  300.6 1.1 copy-start.2
  690.7 6.1 copy-start.1
  696.9 1.0 copy-start.3
  740.7 5.4 copy-start.14
  740.7 75.0 %all-to-all-start.3 = ((bf16[8,1024,384]{2,0,1:T(8,128)(2,1)}), bf16[8,1024,384]{2,0,1:T(8,128)(2,1)}, u32[]{:S(2)}, u32[]{:S(2)}) async-start(bf16[8,1024,384]{2,0,1:T(8,128)(2,1)} %copy.94), calls=%async_computation.3 | async-start | bytes 12582912 | tf_op jit(solution)/shard_map/all_to_all | solution.py:85
  746.3 80.2 %copy-start.9 = (s32[16]{0:T(128)}, s32[16]{0:T(128)S(1)}, u32[]{:S(2)}) copy-start(s32[16]{0:T(128)S(1)} %convert_reduce_fusion.1) | copy-start | bytes 196
  815.7 188.9 %all-to-all-start = ((bf16[4,1024,1024]{2,0,1:T(4,128)(2,1)}), bf16[4,1024,1024]{2,0,1:T(4,128)(2,1)}, u32[]{:S(2)}, u32[]{:S(2)}) async-start(bf16[4,1024,1024]{2,0,1:T(4,128)(2,1)} %copy.72), calls=%async_computation | async-start | bytes 16777216 | tf_op jit(solution)/shard_map/all_to_all | solution.py:66
  820.7 509.5 %all-gather.5.cloned.1.call-start = ((), (), s32[]{:S(2)}) async-start(), calls=%async_computation.5 | async-start | bytes 15728640 | tf_op jit(solution)/shard_map/all_gather | solution.py:86
  826.4 0.7 copy-start.8
  1021.3 0.9 copy-start.5
  1143.7 0.9 copy-start.4
  1245.7 3.8 copy-start.10
  1245.7 3.9 copy-start.15
  1245.7 75.2 %all-to-all-start.1 = ((bf16[4,1024,384]{2,0,1:T(4,128)(2,1)}), bf16[4,1024,384]{2,0,1:T(4,128)(2,1)S(1)}, u32[]{:S(2)}, u32[]{:S(2)}) async-start(bf16[4,1024,384]{2,0,1:T(4,128)(2,1)} %copy.80), calls=%async_computation.1 | async-start | bytes 6291456 | tf_op jit(solution)/shard_map/all_to_all | solution.py:81
  1249.5 195.5 %all-gather.3.cloned.1.call-start = ((), (), s32[]{:S(2)}) async-start(), calls=%async_computation.4 | async-start | bytes 14155776 | tf_op jit(solution)/shard_map/all_gather | solution.py:82
  1458.0 16.6 %copy-start.11 = (bf16[1024,1024]{1,0:T(8,128)(2,1)S(1)}, bf16[1024,1024]{1,0:T(8,128)(2,1)}, u32[]{:S(2)}) copy-start(bf16[1024,1024]{1,0:T(8,128)(2,1)} %param.8) | copy-start | bytes 6291460
Sparse Core Ops, SparseCore 0:
  826.6 122.8 all-gather.4
  1330.3 114.6 all-gather.2
where the time goes:
time: 1520 us; the launch traced here: 1510 us
  other arithmetic  588 us (39%)
  waiting for transfers between devices  570 us (38%)
  matrix products  185 us (12%)
  local copies, waits for them, and re-layouts  130 us (9%)
  starting transfers between devices  21.6 us (1%)
    another operation x18, other arithmetic, compress_tile(): lower_factor = jnp.linalg.cholesky(gram)  335 us
    another operation x11, other arithmetic, compress_tile(): jax.scipy.linalg.solve_triangular(lower_factor, sketched.T, lower=True)  241 us
    all_to_all x1, waiting for transfers between devices, local(): lax.all_to_all(sent_col, 'row', split_axis=1, concat_axis=1, tiled=True)  183 us
    all_to_all x1, waiting for transfers between devices, local(): lax.all_to_all(sent_row, 'col', split_axis=1, concat_axis=1, tiled=True)  177 us
    all_gather x1, waiting for transfers between devices, local(): lax.all_gather(pick_mine(back_row, helpers_row, slots_row, cap_row), 'col...  101 us
    all_to_all x1, waiting for transfers between devices, local(): lax.all_to_all(made_row, 'col', split_axis=1, concat_axis=0, tiled=True)  71.4 us
    reshape x2, local copies, waits for them, and re-layouts, pack_slabs(): return packed.reshape(capacity, owners * slabs.shape[1], slabs.shape[2])  43.2 us
    dot_general x2, matrix products, compress_tile(): sketched = jnp.dot(panel_tile, masked, preferred_element_type=jnp.float32)  39.5 us
  transfers between devices with their start and end apart: 6, of which 5 were waited for; matrix products, arithmetic and copies ran while one was open for 20% of the time, Pallas kernels for 0%

commit v1 on v0

v1 whole, which is shorter than its diff:
```python
import functools

import jax
import jax.numpy as jnp
from jax import lax
from jax.experimental import pallas as pl
from jax.experimental.pallas import tpu as pltpu
from jax.sharding import PartitionSpec as P

NB = 32
HIGH = lax.Precision.HIGHEST
NN = (((1,), (0,)), ((), ()))
NT = (((1,), (1,)), ((), ()))
TN = (((0,), (0,)), ((), ()))


def mm(a, b, dims, precision=None):
    return lax.dot_general(a, b, dims, precision=precision, preferred_element_type=jnp.float32)


def invert_diagonal(blocks):
    nb = blocks[0].shape[0]
    row = lax.broadcasted_iota(jnp.int32, (nb, 2 * nb), 0)
    lane = lax.broadcasted_iota(jnp.int32, (nb, 2 * nb), 1)
    eye = (lane == row + nb).astype(jnp.float32)
    work = [jnp.concatenate([b, eye[:, nb:]], axis=1) for b in blocks]
    for j in range(nb - 1):
        for n, a in enumerate(work):
            pivot_row = a[j : j + 1, :]
            scaled = pivot_row / a[j : j + 1, j : j + 1]
            work[n] = a - jnp.where(row > j, a[:, j : j + 1], 0.0) * scaled
    out = []
    for a in work:
        d = jnp.sum(jnp.where(lane == row, a, 0.0), axis=1, keepdims=True)
        r = lax.rsqrt(d)
        r = r * (1.5 - 0.5 * d * r * r)
        out.append(a[:, nb:] * r)
    return out


def invert_cholesky(z_ref, n, width):
    for j in range(width // NB):
        lo, hi = j * NB, (j + 1) * NB
        inverses = invert_diagonal([z_ref[t, lo:hi, lo:hi] for t in range(n)])
        for t in range(n):
            panel = mm(inverses[t], z_ref[t, lo:hi, :], NN, HIGH)
            z_ref[t, lo:hi, :] = panel
            if hi < width:
                z_ref[t, hi:, :] = z_ref[t, hi:, :] - mm(panel[:, hi:width], panel, TN, HIGH)


def factor_kernel(n_l, n_u, n_col, n_row, *refs):
    place, help_l, rank_l, help_u, rank_u = refs[:5]
    raw_l, raw_u, sk_col, sk_row = refs[5:9]
    got_l = refs[9 : 9 + n_col - 1]
    got_u = refs[9 + n_col - 1 : 9 + n_col + n_row - 2]
    rest = refs[9 + n_col + n_row - 2 :]
    q_out = rest[0]
    w_out = rest[1]
    tile, omega, sketched, z, sem, sem_s = rest[2:]
    my_row, my_col = place[0], place[1]
    width = omega.shape[1]
    order = tile.shape[1]
    n = n_l + n_u
    slab_l, slab_u = order // n_col, order // n_row

    def rows(start, count):
        return pl.ds(pl.multiple_of(start * count, count), count)

    copies = []
    for t in range(n):
        mine = []
        if t < n_l:
            k = t * n_col + my_col
            mine.append(pltpu.make_async_copy(sk_col.at[help_l[k]], omega.at[t], sem_s.at[t]))
            for d in range(n_col):
                j = lax.rem(my_col - d + n_col, n_col)
                src = raw_l.at[k] if d == 0 else got_l[d - 1].at[t]
                mine.append(pltpu.make_async_copy(src, tile.at[t, rows(j, slab_l)], sem.at[t, d]))
        else:
            i = t - n_l
            k = i * n_row + my_row
            mine.append(pltpu.make_async_copy(sk_row.at[help_u[k]], omega.at[t], sem_s.at[t]))
            for d in range(n_row):
                j = jnp.bitwise_xor(my_row, d)
                src = raw_u.at[k] if d == 0 else got_u[d - 1].at[i]
                mine.append(pltpu.make_async_copy(src, tile.at[t, rows(j, slab_u)], sem.at[t, d]))
        for c in mine:
            c.start()
        copies.append(mine)

    row = lax.broadcasted_iota(jnp.int32, (width, width), 0)
    lane = lax.broadcasted_iota(jnp.int32, (width, width), 1)
    eye = (row == lane).astype(jnp.float32)
    sub = lax.broadcasted_iota(jnp.int32, (width, order), 0)
    for t in range(n):
        for c in copies[t]:
            c.wait()
        q = rank_l[t * n_col + my_col] if t < n_l else rank_u[(t - n_l) * n_row + my_row]
        masked = jnp.where(sub < q, omega[t].astype(jnp.float32), 0.0).astype(jnp.bfloat16)
        sketched[t] = mm(masked, tile[t], NT)
        gram = mm(sketched[t], sketched[t], NT, HIGH) + jnp.where(row >= q, eye, 0.0)
        z[t] = jnp.concatenate([gram, eye], axis=1)
    invert_cholesky(z, n, width)
    for t in range(n):
        basis = mm(z[t, :, width:], sketched[t], NN, HIGH).astype(jnp.bfloat16)
        q_out[t] = basis
        w_out[t] = mm(basis, tile[t], NN).astype(jnp.bfloat16)


def factor(place, help_l, rank_l, help_u, rank_u, raw_l, raw_u, sk_col, sk_row, got_l, got_u):
    n_col, n_row = len(got_l) + 1, len(got_u) + 1
    n_l, n_u = raw_l.shape[0] // n_col, raw_u.shape[0] // n_row
    n = n_l + n_u
    width, order = sk_col.shape[1:]
    smem = pl.BlockSpec(memory_space=pltpu.SMEM)
    hbm = pl.BlockSpec(memory_space=pl.ANY)
    vmem = pl.BlockSpec(memory_space=pltpu.VMEM)
    made = jax.ShapeDtypeStruct((n, width, order), jnp.bfloat16)
    return pl.pallas_call(
        functools.partial(factor_kernel, n_l, n_u, n_col, n_row),
        out_shape=(made, made),
        in_specs=[smem] * 5 + [hbm] * (4 + n_col + n_row - 2),
        out_specs=(vmem, vmem),
        scratch_shapes=[
            pltpu.VMEM((n, order, order), jnp.bfloat16),
            pltpu.VMEM((n, width, order), jnp.bfloat16),
            pltpu.VMEM((n, width, order), jnp.float32),
            pltpu.VMEM((n, width, 2 * width), jnp.float32),
            pltpu.SemaphoreType.DMA((n, max(n_col, n_row))),
            pltpu.SemaphoreType.DMA((n,)),
        ],
        compiler_params=pltpu.CompilerParams(vmem_limit_bytes=56 * 2**20),
        name="factor_tiles",
    )(place, help_l, rank_l, help_u, rank_u, raw_l, raw_u, sk_col, sk_row, *got_l, *got_u)


def update_kernel(n_l, n_u, n_col, n_row, group, *refs):
    place, trailing = refs[:2]
    at = 2
    lq = refs[at : at + n_col]
    at += n_col
    lw = refs[at : at + n_col]
    at += n_col
    uq = refs[at : at + 2 * n_row]
    at += 2 * n_row
    uw = refs[at : at + 2 * n_row]
    at += 2 * n_row
    out, ql, wl, qu, wu, left, sem, sem_t, tr = refs[at:]
    my_row, my_col = place[0], place[1]
    width = ql.shape[1]
    chips = n_col // 2
    chip, core = my_col // 2, lax.rem(my_col, 2)
    half = n_u // 2
    depth = n_l * n_col
    load = pltpu.make_async_copy(trailing, tr, sem_t)
    load.start()

    def start_l(i):
        for s in range(chips):
            for x in range(2):
                f = 2 * lax.rem(chip - s + chips, chips) + jnp.bitwise_xor(core, x)
                k = i * n_col + f
                pltpu.make_async_copy(lw[2 * s + x].at[i], wl.at[k], sem.at[1, k]).start()
                pltpu.make_async_copy(lq[2 * s + x].at[i], ql.at[k], sem.at[0, k]).start()

    def start_u(j):
        for o in range(n_row):
            k = j * n_row + jnp.bitwise_xor(my_row, o)
            src = 2 * o + j // half
            pltpu.make_async_copy(uq[src].at[j % half], qu.at[k], sem.at[2, k]).start()
            pltpu.make_async_copy(uw[src].at[j % half], wu.at[k], sem.at[3, k]).start()

    per = n_u // n_l
    for i in range(n_l):
        for j in range(i * per, (i + 1) * per):
            start_u(j)
        start_l(i)
    load.wait()
    out[...] = tr[...].astype(jnp.float32)

    def one_group(g, carry):
        for e in range(group):
            k = g * group + e
            for a, buf in enumerate((ql, wl, qu, wu)):
                pltpu.make_async_copy(buf.at[k], buf.at[k], sem.at[a, k]).wait()
            mid = mm(qu[k], wl[k], NT).astype(jnp.bfloat16)
            left[e * width : (e + 1) * width, :] = mm(mid, ql[k], NN).astype(jnp.bfloat16)
        coeff = wu[pl.ds(g * group, group)].reshape(group * width, wu.shape[2])
        out[...] = out[...] - mm(left[...], coeff, TN)
        return carry

    lax.fori_loop(0, depth // group, one_group, 0)


def update(place, trailing, lq, lw, uq, uw, n_l, n_u):
    n_col, n_row = len(lq), len(uq) // 2
    depth = n_l * n_col
    width, order = lq[0].shape[1:]
    group = 4
    smem = pl.BlockSpec(memory_space=pltpu.SMEM)
    hbm = pl.BlockSpec(memory_space=pl.ANY)
    vmem = pl.BlockSpec(memory_space=pltpu.VMEM)
    held = pltpu.VMEM((depth, width, order), jnp.bfloat16)
    return pl.pallas_call(
        functools.partial(update_kernel, n_l, n_u, n_col, n_row, group),
        out_shape=jax.ShapeDtypeStruct(trailing.shape, jnp.float32),
        in_specs=[smem] + [hbm] * (1 + 2 * n_col + 4 * n_row),
        out_specs=vmem,
        scratch_shapes=[held, held, held, held]
        + [
            pltpu.VMEM((group * width, order), jnp.bfloat16),
            pltpu.SemaphoreType.DMA((4, depth)),
            pltpu.SemaphoreType.DMA,
            pltpu.VMEM(trailing.shape, trailing.dtype),
        ],
        compiler_params=pltpu.CompilerParams(vmem_limit_bytes=56 * 2**20),
        name="update_tile",
    )(place, trailing, *lq, *lw, *uq, *uw)


def shift(x, axis, size, move):
    return lax.ppermute(x, axis, [(i, move(i)) for i in range(size)])


def exchange_l(raw, n_col):
    me = lax.axis_index("col")
    x = raw.reshape((-1, n_col) + raw.shape[1:])
    return [
        shift(
            lax.dynamic_index_in_dim(x, lax.rem(me + d, n_col), 1, False),
            "col",
            n_col,
            lambda i: (i + d) % n_col,
        )
        for d in range(1, n_col)
    ]


def exchange_u(raw, n_row):
    me = lax.axis_index("row")
    x = raw.reshape((-1, n_row) + raw.shape[1:])
    return [
        shift(
            lax.dynamic_index_in_dim(x, jnp.bitwise_xor(me, d), 1, False),
            "row",
            n_row,
            lambda i: i ^ d,
        )
        for d in range(1, n_row)
    ]


def gather_col(pieces, n_col):
    chips = n_col // 2
    out = [[] for _ in pieces]
    now = list(pieces)
    for s in range(chips):
        later = [shift(p, "col", n_col, lambda i: (i + 2) % n_col) for p in now] if s + 1 < chips else []
        for o, p in zip(out, now):
            o += [p, shift(p, "col", n_col, lambda i: i ^ 1)]
        now = later
    return out


def gather_row(pieces, n_row):
    bits = [1 << b for b in range(n_row.bit_length() - 1)]
    out = []
    for number, piece in enumerate(pieces):
        turn = number % len(bits)
        held = {0: piece}
        for b in bits[turn:] + bits[:turn]:
            held.update({o ^ b: shift(p, "row", n_row, lambda i: i ^ b) for o, p in held.items()})
        out.append([held[o] for o in range(n_row)])
    return out


def local(trailing, raw_l, raw_u, sketch, helper_l, helper_u, ranks_l, ranks_u):
    n_col, n_row = lax.axis_size("col"), lax.axis_size("row")
    place = jnp.stack([lax.axis_index("row"), lax.axis_index("col")]).astype(jnp.int32)
    mine_l, mine_u = raw_l[0], raw_u[:, 0]
    n_l, n_u = mine_l.shape[0] // n_col, mine_u.shape[0] // n_row
    own = jnp.swapaxes(sketch[0, 0], 0, 1)[None]
    sk_col = lax.all_gather(own, "col", axis=0, tiled=True)
    sk_row = lax.all_gather(own, "row", axis=0, tiled=True)
    got_l = exchange_l(mine_l, n_col)
    got_u = exchange_u(mine_u, n_row)
    q, w = factor(
        place, helper_l[0], ranks_l[0], helper_u[:, 0], ranks_u[:, 0],
        mine_l, mine_u, sk_col, sk_row, got_l, got_u,
    )
    half = n_l + n_u // 2
    lq, lw = gather_col([q[:n_l], w[:n_l]], n_col)
    parts = gather_row([q[n_l:half], q[half:], w[n_l:half], w[half:]], n_row)
    uq = [p for pair in zip(parts[0], parts[1]) for p in pair]
    uw = [p for pair in zip(parts[2], parts[3]) for p in pair]
    return update(place, trailing, lq, lw, uq, uw, n_l, n_u)


def solution(mesh):
    placed = (
        P("row", "col"),
        P("row", None, "col", None),
        P(None, "col", "row", None),
        P("row", "col", None, None),
        P("row", None),
        P(None, "col"),
        P("row", None),
        P(None, "col"),
    )
    return jax.shard_map(
        local, mesh=mesh, in_specs=placed, out_specs=P("row", "col"), check_vma=False
    )
```

time: 1520 us -> 375 us (0.25)
  other arithmetic: 588 us -> 0.67 us
  waiting for transfers between devices: 570 us -> 240 us
  matrix products: 185 us -> 0 us
  local copies, waits for them, and re-layouts: 130 us -> 12.4 us
  Pallas kernels: 0 us -> 77.8 us
    another operation x29 -> x1, other arithmetic: 576 us -> 0.67 us  [local(): jnp.stack([lax.axis_index('row'), lax.axis_index('col')]).astype(jnp.int32)]
    all_to_all x4 -> x0, waiting for transfers between devices: 469 us -> none  [the longest x1 183 us: local(): lax.all_to_all(sent_col, 'row', split_axis=1, concat_axis=1, tiled=True)]
    ppermute x0 -> x36, waiting for transfers between devices: none -> 222 us  [shift(): return lax.ppermute(x, axis, [(i, move(i)) for i in range(size)])]
    dot_general x12 -> x0, matrix products: 158 us -> none  [the longest x2 39.5 us: compress_tile(): sketched = jnp.dot(panel_tile, masked, preferred_element_type=jnp.float32)]
    all_gather x2, waiting for transfers between devices: 101 us -> 16.8 us  [the longest x1 16.8 us: local(): sk_col = lax.all_gather(own, 'col', axis=0, tiled=True)]
    pallas_call x0 -> x2, Pallas kernels: none -> 77.8 us  [the longest x1 48.6 us: factor(): pl.pallas_call(functools.partial(factor_kernel, n_l, n_u, n_col, n_row),...]
    reshape x2 -> x0, local copies, waits for them, and re-layouts: 43.2 us -> none  [pack_slabs(): return packed.reshape(capacity, owners * slabs.shape[1], slabs.shape[2])]
    ppermute x0 -> x36, starting transfers between devices: none -> 27.8 us  [shift(): return lax.ppermute(x, axis, [(i, move(i)) for i in range(size)])]
  transfers between devices with their start and end apart: 6 -> 38, of which waited for: 5 -> 21; matrix products, arithmetic and copies ran while one was open for 20% -> 2% of each run, Pallas kernels for 0% -> 0%
where the time goes in v1:
time: 375 us; the launch traced here: 373 us
  waiting for transfers between devices  240 us (64%)
  Pallas kernels  77.8 us (21%)
  starting transfers between devices  27.9 us (7%)
  between operations  14.4 us (4%)
  local copies, waits for them, and re-layouts  12.4 us (3%)
    ppermute x36, waiting for transfers between devices, shift(): return lax.ppermute(x, axis, [(i, move(i)) for i in range(size)])  222 us
    pallas_call x1, Pallas kernels, factor(): pl.pallas_call(functools.partial(factor_kernel, n_l, n_u, n_col, n_row),...  48.6 us
    pallas_call x1, Pallas kernels, update(): pl.pallas_call(functools.partial(update_kernel, n_l, n_u, n_col, n_row, g...  29.2 us
    ppermute x36, starting transfers between devices, shift(): return lax.ppermute(x, axis, [(i, move(i)) for i in range(size)])  27.8 us
    all_gather x1, waiting for transfers between devices, local(): sk_col = lax.all_gather(own, 'col', axis=0, tiled=True)  16.8 us
  transfers between devices with their start and end apart: 38, of which 21 were waited for; matrix products, arithmetic and copies ran while one was open for 2% of the time, Pallas kernels for 0%

profile of v1, /device:TPU:0, one launch (start us, length us, event | category | flops | bytes accessed | tf_op | source)
XLA Modules:
  0.0 373.1 jit_solution(4415464850401782012)
XLA Ops:
  8.0 3.7 dynamic-slice_bitcast_fusion.3
  11.7 4.5 %collective-permute-start.6 = (bf16[2,128,1024]{2,1,0:T(8,128)(2,1)}, bf16[2,128,1024]{2,1,0:T(8,128)(2,1)S(1)}, u32[]{:S(2)}, u32[]{:S(2)}) collective-permute-start(bf16[2,128,1024]{2,1,0:T(8,128)(2,1)} %get-tuple-element.12), channel_id=1, source_target_pairs={{0,7},{1,0},{2,1},{3,2},{4,3},{5,4},{6,5},{7,6},{8,15},{9,8},{10,9... | collective-permute-start | bytes 1572872 | tf_op jit(solution)/shard_map/ppermute | solution.py:223
  16.3 3.9 %dynamic-slice_bitcast_fusion = (bf16[4,256,1024]{2,1,0:T(8,128)(2,1)S(1)}, bf16[4,256,1024]{2,1,0:T(8,128)(2,1)S(1)}, bf16[4,256,1024]{2,1,0:T(8,128)(2,1)S(1)}) fusion(bf16[4,4,256,1024]{3,2,1,0:T(8,128)(2,1)} %bitcast.55, s32[]{:T(128)S(6)} %select_n.41, s32[]{:T(128)S(6)} %select_n.40, s32[]{:T(128)S(6)} %select_n.39), kind=kLoop, calls=%fused_computation | loop fusion | bytes 12582924 | tf_op jit(solution)/shard_map/jit(dynamic_index_in_dim)/squeeze | solution.py:245
  24.4 15.2 %collective-permute-done.5.refs_14_ = bf16[2,128,1024]{2,1,0:T(8,128)(2,1)S(1)} collective-permute-done((bf16[2,128,1024]{2,1,0:T(8,128)(2,1)S(1)}, bf16[2,128,1024]{2,1,0:T(8,128)(2,1)S(1)}, u32[]{:S(2)}, u32[]{:S(2)}) %collective-permute-start.5) | collective-permute-done | bytes 524320 | tf_op jit(solution)/shard_map/ppermute | solution.py:223
  39.7 8.1 %collective-permute-done.4.refs_13_ = bf16[2,128,1024]{2,1,0:T(8,128)(2,1)S(1)} collective-permute-done((bf16[2,128,1024]{2,1,0:T(8,128)(2,1)S(1)}, bf16[2,128,1024]{2,1,0:T(8,128)(2,1)S(1)}, u32[]{:S(2)}, u32[]{:S(2)}) %collective-permute-start.4) | collective-permute-done | bytes 524320 | tf_op jit(solution)/shard_map/ppermute | solution.py:223
  49.0 43.6 %collective-permute-done.3.refs_12_ = bf16[2,128,1024]{2,1,0:T(8,128)(2,1)S(1)} collective-permute-done((bf16[2,128,1024]{2,1,0:T(8,128)(2,1)S(1)}, bf16[2,128,1024]{2,1,0:T(8,128)(2,1)S(1)}, u32[]{:S(2)}, u32[]{:S(2)}) %collective-permute-start.3) | collective-permute-done | bytes 524320 | tf_op jit(solution)/shard_map/ppermute | solution.py:223
  92.6 4.2 %collective-permute-done.2.refs_11_ = bf16[2,128,1024]{2,1,0:T(8,128)(2,1)S(1)} collective-permute-done((bf16[2,128,1024]{2,1,0:T(8,128)(2,1)S(1)}, bf16[2,128,1024]{2,1,0:T(8,128)(2,1)S(1)}, u32[]{:S(2)}, u32[]{:S(2)}) %collective-permute-start.2) | collective-permute-done | bytes 524320 | tf_op jit(solution)/shard_map/ppermute | solution.py:223
  97.6 6.9 %collective-permute-done.1.refs_10_ = bf16[2,128,1024]{2,1,0:T(8,128)(2,1)S(1)} collective-permute-done((bf16[2,128,1024]{2,1,0:T(8,128)(2,1)S(1)}, bf16[2,128,1024]{2,1,0:T(8,128)(2,1)S(1)}, u32[]{:S(2)}, u32[]{:S(2)}) %collective-permute-start.1) | collective-permute-done | bytes 524320 | tf_op jit(solution)/shard_map/ppermute | solution.py:223
  104.6 4.6 %collective-permute-done.refs_9_ = bf16[2,128,1024]{2,1,0:T(8,128)(2,1)S(1)} collective-permute-done((bf16[2,128,1024]{2,1,0:T(8,128)(2,1)S(1)}, bf16[2,128,1024]{2,1,0:T(8,128)(2,1)S(1)}, u32[]{:S(2)}, u32[]{:S(2)}) %collective-permute-start) | collective-permute-done | bytes 524320 | tf_op jit(solution)/shard_map/ppermute | solution.py:223
  109.2 14.3 %collective-permute-done.8.refs_17_ = bf16[4,256,1024]{2,1,0:T(8,128)(2,1)} collective-permute-done((bf16[4,256,1024]{2,1,0:T(8,128)(2,1)S(1)}, bf16[4,256,1024]{2,1,0:T(8,128)(2,1)}, u32[]{:S(2)}, u32[]{:S(2)}) %collective-permute-start.8) | collective-permute-done | bytes 2097184 | tf_op jit(solution)/shard_map/ppermute | solution.py:223
  123.7 16.8 %all-gather.5.cloned.1.call-done = bf16[1536,1024]{1,0:T(8,128)(2,1)} async-done(((bf16[192,1024]{1,0:T(8,128)(2,1)}), bf16[1536,1024]{1,0:T(8,128)(2,1)}) %all-gather.5.cloned.1.call-update) | async-done | bytes 3145744 | tf_op jit(solution)/shard_map/all_gather | solution.py:284
  140.5 48.6 %factor_tiles.1 = (bf16[6,192,1024]{2,1,0:T(8,128)(2,1)}, bf16[6,192,1024]{2,1,0:T(8,128)(2,1)}) custom-call(s32[2]{0:T(128)} %pad_add_fusion.refs_0_, s32[16]{0:T(128)} %bitcast.63, s32[16]{0:T(128)} %bitcast.64, s32[16]{0:T(128)} %bitcast.65, s32[16]{0:T(128)} %bitcast.66, bf16[16,128,1024]{2,1,0:T(8,128)(2,1)} %bitcast.58, ...), custom_call_target="tpu_custom_call" | custom-call | tf_op jit(solution)/shard_map/factor_tiles/pallas_call | solution.py:120
  195.9 15.8 %collective-permute-done.27.refs_23_ = bf16[2,192,1024]{2,1,0:T(8,128)(2,1)S(1)} collective-permute-done((bf16[2,192,1024]{2,1,0:T(8,128)(2,1)S(1)}, bf16[2,192,1024]{2,1,0:T(8,128)(2,1)S(1)}, u32[]{:S(2)}, u32[]{:S(2)}) %collective-permute-start.27) | collective-permute-done | bytes 786464 | tf_op jit(solution)/shard_map/ppermute | solution.py:223
  213.8 14.8 %collective-permute-done.26.refs_22_ = bf16[2,192,1024]{2,1,0:T(8,128)(2,1)S(1)} collective-permute-done((bf16[2,192,1024]{2,1,0:T(8,128)(2,1)S(1)}, bf16[2,192,1024]{2,1,0:T(8,128)(2,1)S(1)}, u32[]{:S(2)}, u32[]{:S(2)}) %collective-permute-start.26) | collective-permute-done | bytes 786464 | tf_op jit(solution)/shard_map/ppermute | solution.py:223
  232.6 12.8 %collective-permute-done.33.refs_31_ = bf16[2,192,1024]{2,1,0:T(8,128)(2,1)S(1)} collective-permute-done((bf16[2,192,1024]{2,1,0:T(8,128)(2,1)S(1)}, bf16[2,192,1024]{2,1,0:T(8,128)(2,1)S(1)}, u32[]{:S(2)}, u32[]{:S(2)}) %collective-permute-start.33) | collective-permute-done | bytes 786464 | tf_op jit(solution)/shard_map/ppermute | solution.py:223
  245.4 3.6 collective-permute-done.31.refs_29_
  250.5 11.1 %collective-permute-done.32.refs_30_ = bf16[2,192,1024]{2,1,0:T(8,128)(2,1)S(1)} collective-permute-done((bf16[2,192,1024]{2,1,0:T(8,128)(2,1)S(1)}, bf16[2,192,1024]{2,1,0:T(8,128)(2,1)S(1)}, u32[]{:S(2)}, u32[]{:S(2)}) %collective-permute-start.32) | collective-permute-done | bytes 786464 | tf_op jit(solution)/shard_map/ppermute | solution.py:223
  263.0 2.8 collective-permute-done.30.refs_28_
  267.7 12.7 %collective-permute-done.29.refs_25_ = bf16[2,192,1024]{2,1,0:T(8,128)(2,1)S(1)} collective-permute-done((bf16[2,192,1024]{2,1,0:T(8,128)(2,1)S(1)}, bf16[2,192,1024]{2,1,0:T(8,128)(2,1)S(1)}, u32[]{:S(2)}, u32[]{:S(2)}) %collective-permute-start.29) | collective-permute-done | bytes 786464 | tf_op jit(solution)/shard_map/ppermute | solution.py:223
  283.4 4.7 %collective-permute-done.13.refs_6_ = bf16[2,192,1024]{2,1,0:T(8,128)(2,1)S(1)} collective-permute-done((bf16[2,192,1024]{2,1,0:T(8,128)(2,1)S(1)}, bf16[2,192,1024]{2,1,0:T(8,128)(2,1)S(1)}, u32[]{:S(2)}, u32[]{:S(2)}) %collective-permute-start.13) | collective-permute-done | bytes 786464 | tf_op jit(solution)/shard_map/ppermute | solution.py:223
  288.2 16.8 %collective-permute-done.20.refs_14_ = bf16[2,192,1024]{2,1,0:T(8,128)(2,1)S(1)} collective-permute-done((bf16[2,192,1024]{2,1,0:T(8,128)(2,1)S(1)}, bf16[2,192,1024]{2,1,0:T(8,128)(2,1)S(1)}, u32[]{:S(2)}, u32[]{:S(2)}) %collective-permute-start.20) | collective-permute-done | bytes 786464 | tf_op jit(solution)/shard_map/ppermute | solution.py:223
  305.8 16.1 %collective-permute-done.15.refs_8_ = bf16[2,192,1024]{2,1,0:T(8,128)(2,1)S(1)} collective-permute-done((bf16[2,192,1024]{2,1,0:T(8,128)(2,1)S(1)}, bf16[2,192,1024]{2,1,0:T(8,128)(2,1)S(1)}, u32[]{:S(2)}, u32[]{:S(2)}) %collective-permute-start.15) | collective-permute-done | bytes 786464 | tf_op jit(solution)/shard_map/ppermute | solution.py:223
  321.9 12.1 %collective-permute-done.22.refs_16_ = bf16[2,192,1024]{2,1,0:T(8,128)(2,1)S(1)} collective-permute-done((bf16[2,192,1024]{2,1,0:T(8,128)(2,1)S(1)}, bf16[2,192,1024]{2,1,0:T(8,128)(2,1)S(1)}, u32[]{:S(2)}, u32[]{:S(2)}) %collective-permute-start.22) | collective-permute-done | bytes 786464 | tf_op jit(solution)/shard_map/ppermute | solution.py:223
  336.6 29.2 %update_tile.1 = f32[1024,1024]{1,0:T(8,128)} custom-call(s32[2]{0:T(128)} %pad_add_fusion.refs_0_, bf16[1024,1024]{1,0:T(8,128)(2,1)} %refs_1_.1, bf16[2,192,1024]{2,1,0:T(8,128)(2,1)} %copy-done.2, bf16[2,192,1024]{2,1,0:T(8,128)(2,1)} %copy-done.13, bf16[2,192,1024]{2,1,0:T(8,128)(2,1)} %copy-done.12, bf16[2,192,1024]{2,1,0:T(8,128)(2,1)} %copy-done.24, ...), custom_call_target="tpu_custom_call" | custom-call | tf_op jit(solution)/shard_map/update_tile/pallas_call | solution.py:205
  (151 shorter events, 31.8 us)
Async XLA Ops:
  6.5 117.2 %all-gather.7.cloned.1.call-start = ((), (), s32[]{:S(2)}) async-start(), calls=%async_computation.1 | async-start | bytes 1966080 | tf_op jit(solution)/shard_map/all_gather | solution.py:285
  7.3 133.2 %all-gather.5.cloned.1.call-start = ((), (), s32[]{:S(2)}) async-start(), calls=%async_computation | async-start | bytes 3538944 | tf_op jit(solution)/shard_map/all_gather | solution.py:284
  20.2 89.0 %collective-permute-start.9 = (bf16[4,256,1024]{2,1,0:T(8,128)(2,1)S(1)}, bf16[4,256,1024]{2,1,0:T(8,128)(2,1)S(1)}, u32[]{:S(2)}, u32[]{:S(2)}) collective-permute-start(bf16[4,256,1024]{2,1,0:T(8,128)(2,1)S(1)} %get-tuple-element.9), channel_id=1, source_target_pairs={{0,24},{8,16},{16,8},{24,0},{1,25},{9,17},{17,9},{25,1},{2,26},{10... | collective-permute-start | bytes 6291464 | tf_op jit(solution)/shard_map/ppermute | solution.py:223
  22.6 100.8 %collective-permute-start.8 = (bf16[4,256,1024]{2,1,0:T(8,128)(2,1)S(1)}, bf16[4,256,1024]{2,1,0:T(8,128)(2,1)}, u32[]{:S(2)}, u32[]{:S(2)}) collective-permute-start(bf16[4,256,1024]{2,1,0:T(8,128)(2,1)S(1)} %get-tuple-element.10), channel_id=1, source_target_pairs={{0,16},{8,24},{16,0},{24,8},{1,17},{9,25},{17,1},{25,9},{2,18},{10... | collective-permute-start | bytes 6291464 | tf_op jit(solution)/shard_map/ppermute | solution.py:223
  23.1 100.6 %collective-permute-start.7 = (bf16[4,256,1024]{2,1,0:T(8,128)(2,1)S(1)}, bf16[4,256,1024]{2,1,0:T(8,128)(2,1)}, u32[]{:S(2)}, u32[]{:S(2)}) collective-permute-start(bf16[4,256,1024]{2,1,0:T(8,128)(2,1)S(1)} %get-tuple-element.11), channel_id=1, source_target_pairs={{0,8},{8,0},{16,24},{24,16},{1,9},{9,1},{17,25},{25,17},{2,10},{10... | collective-permute-start | bytes 6291464 | tf_op jit(solution)/shard_map/ppermute | solution.py:223
  39.6 52.9 %collective-permute-start.3 = (bf16[2,128,1024]{2,1,0:T(8,128)(2,1)S(1)}, bf16[2,128,1024]{2,1,0:T(8,128)(2,1)S(1)}, u32[]{:S(2)}, u32[]{:S(2)}) collective-permute-start(bf16[2,128,1024]{2,1,0:T(8,128)(2,1)S(1)} %copy-done.36), channel_id=1, source_target_pairs={{0,4},{1,5},{2,6},{3,7},{4,0},{5,1},{6,2},{7,3},{8,12},{9,13},{10,... | collective-permute-start | bytes 1572872 | tf_op jit(solution)/shard_map/ppermute | solution.py:223
  47.8 49.0 %collective-permute-start.2 = (bf16[2,128,1024]{2,1,0:T(8,128)(2,1)S(1)}, bf16[2,128,1024]{2,1,0:T(8,128)(2,1)S(1)}, u32[]{:S(2)}, u32[]{:S(2)}) collective-permute-start(bf16[2,128,1024]{2,1,0:T(8,128)(2,1)S(1)} %copy-done.35), channel_id=1, source_target_pairs={{0,3},{1,4},{2,5},{3,6},{4,7},{5,0},{6,1},{7,2},{8,11},{9,12},{10,... | collective-permute-start | bytes 1572872 | tf_op jit(solution)/shard_map/ppermute | solution.py:223
  194.3 34.3 %collective-permute-start.26 = (bf16[2,192,1024]{2,1,0:T(8,128)(2,1)S(1)}, bf16[2,192,1024]{2,1,0:T(8,128)(2,1)S(1)}, u32[]{:S(2)}, u32[]{:S(2)}) collective-permute-start(bf16[2,192,1024]{2,1,0:T(8,128)(2,1)S(1)} %get-tuple-element.23.refs_18_), channel_id=1, source_target_pairs={{0,16},{8,24},{16,0},{24,8},{1,17},{9,25},{17,1},{25,9},{2,18},{10... | collective-permute-start | bytes 2359304 | tf_op jit(solution)/shard_map/ppermute | solution.py:223
  194.8 35.2 %collective-permute-start.24 = (bf16[2,192,1024]{2,1,0:T(8,128)(2,1)S(1)}, bf16[2,192,1024]{2,1,0:T(8,128)(2,1)S(1)}, u32[]{:S(2)}, u32[]{:S(2)}) collective-permute-start(bf16[2,192,1024]{2,1,0:T(8,128)(2,1)S(1)} %get-tuple-element.23.refs_18_), channel_id=1, source_target_pairs={{0,8},{8,0},{16,24},{24,16},{1,9},{9,1},{17,25},{25,17},{2,10},{10... | collective-permute-start | bytes 2359304 | tf_op jit(solution)/shard_map/ppermute | solution.py:223
  195.4 36.1 %collective-permute-start.11 = (bf16[2,192,1024]{2,1,0:T(8,128)(2,1)S(1)}, bf16[2,192,1024]{2,1,0:T(8,128)(2,1)S(1)}, u32[]{:S(2)}, u32[]{:S(2)}) collective-permute-start(bf16[2,192,1024]{2,1,0:T(8,128)(2,1)S(1)} %get-tuple-element.24.refs_2_), channel_id=1, source_target_pairs={{0,2},{1,3},{2,4},{3,5},{4,6},{5,7},{6,0},{7,1},{8,10},{9,11},{10,... | collective-permute-start | bytes 2359304 | tf_op jit(solution)/shard_map/ppermute | solution.py:223
  213.2 32.2 %collective-permute-start.33 = (bf16[2,192,1024]{2,1,0:T(8,128)(2,1)S(1)}, bf16[2,192,1024]{2,1,0:T(8,128)(2,1)S(1)}, u32[]{:S(2)}, u32[]{:S(2)}) collective-permute-start(bf16[2,192,1024]{2,1,0:T(8,128)(2,1)S(1)} %get-tuple-element.19.refs_27_), channel_id=1, source_target_pairs={{0,16},{8,24},{16,0},{24,8},{1,17},{9,25},{17,1},{25,9},{2,18},{10... | collective-permute-start | bytes 2359304 | tf_op jit(solution)/shard_map/ppermute | solution.py:223
  230.0 31.5 %collective-permute-start.32 = (bf16[2,192,1024]{2,1,0:T(8,128)(2,1)S(1)}, bf16[2,192,1024]{2,1,0:T(8,128)(2,1)S(1)}, u32[]{:S(2)}, u32[]{:S(2)}) collective-permute-start(bf16[2,192,1024]{2,1,0:T(8,128)(2,1)S(1)} %get-tuple-element.20.refs_26_), channel_id=1, source_target_pairs={{0,16},{8,24},{16,0},{24,8},{1,17},{9,25},{17,1},{25,9},{2,18},{10... | collective-permute-start | bytes 2359304 | tf_op jit(solution)/shard_map/ppermute | solution.py:223
  231.5 34.4 %collective-permute-start.30 = (bf16[2,192,1024]{2,1,0:T(8,128)(2,1)S(1)}, bf16[2,192,1024]{2,1,0:T(8,128)(2,1)S(1)}, u32[]{:S(2)}, u32[]{:S(2)}) collective-permute-start(bf16[2,192,1024]{2,1,0:T(8,128)(2,1)S(1)} %get-tuple-element.20.refs_26_), channel_id=1, source_target_pairs={{0,8},{8,0},{16,24},{24,16},{1,9},{9,1},{17,25},{25,17},{2,10},{10... | collective-permute-start | bytes 2359304 | tf_op jit(solution)/shard_map/ppermute | solution.py:223
  232.1 34.3 %collective-permute-start.18 = (bf16[2,192,1024]{2,1,0:T(8,128)(2,1)S(1)}, bf16[2,192,1024]{2,1,0:T(8,128)(2,1)S(1)}, u32[]{:S(2)}, u32[]{:S(2)}) collective-permute-start(bf16[2,192,1024]{2,1,0:T(8,128)(2,1)S(1)} %get-tuple-element.21.refs_10_), channel_id=1, source_target_pairs={{0,2},{1,3},{2,4},{3,5},{4,6},{5,7},{6,0},{7,1},{8,10},{9,11},{10,... | collective-permute-start | bytes 2359304 | tf_op jit(solution)/shard_map/ppermute | solution.py:223
  249.0 31.4 %collective-permute-start.29 = (bf16[2,192,1024]{2,1,0:T(8,128)(2,1)S(1)}, bf16[2,192,1024]{2,1,0:T(8,128)(2,1)S(1)}, u32[]{:S(2)}, u32[]{:S(2)}) collective-permute-start(bf16[2,192,1024]{2,1,0:T(8,128)(2,1)S(1)} %collective-permute-done.27.refs_23_), channel_id=1, source_target_pairs={{0,8},{8,0},{16,24},{24,16},{1,9},{9,1},{17,25},{25,17},{2,10},{10... | collective-permute-start | bytes 2359304 | tf_op jit(solution)/shard_map/ppermute | solution.py:223
  266.4 38.6 %collective-permute-start.20 = (bf16[2,192,1024]{2,1,0:T(8,128)(2,1)S(1)}, bf16[2,192,1024]{2,1,0:T(8,128)(2,1)S(1)}, u32[]{:S(2)}, u32[]{:S(2)}) collective-permute-start(bf16[2,192,1024]{2,1,0:T(8,128)(2,1)S(1)} %collective-permute-done.18.refs_12_), channel_id=1, source_target_pairs={{0,2},{1,3},{2,4},{3,5},{4,6},{5,7},{6,0},{7,1},{8,10},{9,11},{10,... | collective-permute-start | bytes 2359304 | tf_op jit(solution)/shard_map/ppermute | solution.py:223
  267.7 37.3 %collective-permute-start.12 = (bf16[2,192,1024]{2,1,0:T(8,128)(2,1)S(1)}, bf16[2,192,1024]{2,1,0:T(8,128)(2,1)S(1)}, u32[]{:S(2)}, u32[]{:S(2)}) collective-permute-start(bf16[2,192,1024]{2,1,0:T(8,128)(2,1)S(1)} %collective-permute-done.11.refs_4_), channel_id=1, source_target_pairs={{0,1},{1,0},{2,3},{3,2},{4,5},{5,4},{6,7},{7,6},{8,9},{9,8},{10,11... | collective-permute-start | bytes 2359304 | tf_op jit(solution)/shard_map/ppermute | solution.py:223
  280.4 24.7 %collective-permute-start.35 = (bf16[2,192,1024]{2,1,0:T(8,128)(2,1)S(1)}, bf16[2,192,1024]{2,1,0:T(8,128)(2,1)S(1)}, u32[]{:S(2)}, u32[]{:S(2)}) collective-permute-start(bf16[2,192,1024]{2,1,0:T(8,128)(2,1)S(1)} %collective-permute-done.33.refs_31_), channel_id=1, source_target_pairs={{0,8},{8,0},{16,24},{24,16},{1,9},{9,1},{17,25},{25,17},{2,10},{10... | collective-permute-start | bytes 2359304 | tf_op jit(solution)/shard_map/ppermute | solution.py:223
  281.9 23.8 %collective-permute-start.34 = (bf16[2,192,1024]{2,1,0:T(8,128)(2,1)S(1)}, bf16[2,192,1024]{2,1,0:T(8,128)(2,1)S(1)}, u32[]{:S(2)}, u32[]{:S(2)}) collective-permute-start(bf16[2,192,1024]{2,1,0:T(8,128)(2,1)S(1)} %collective-permute-done.30.refs_28_), channel_id=1, source_target_pairs={{0,16},{8,24},{16,0},{24,8},{1,17},{9,25},{17,1},{25,9},{2,18},{10... | collective-permute-start | bytes 2359304 | tf_op jit(solution)/shard_map/ppermute | solution.py:223
  288.2 33.7 %collective-permute-start.15 = (bf16[2,192,1024]{2,1,0:T(8,128)(2,1)S(1)}, bf16[2,192,1024]{2,1,0:T(8,128)(2,1)S(1)}, u32[]{:S(2)}, u32[]{:S(2)}) collective-permute-start(bf16[2,192,1024]{2,1,0:T(8,128)(2,1)S(1)} %collective-permute-done.13.refs_6_), channel_id=1, source_target_pairs={{0,2},{1,3},{2,4},{3,5},{4,6},{5,7},{6,0},{7,1},{8,10},{9,11},{10,... | collective-permute-start | bytes 2359304 | tf_op jit(solution)/shard_map/ppermute | solution.py:223
  305.0 29.0 %collective-permute-start.22 = (bf16[2,192,1024]{2,1,0:T(8,128)(2,1)S(1)}, bf16[2,192,1024]{2,1,0:T(8,128)(2,1)S(1)}, u32[]{:S(2)}, u32[]{:S(2)}) collective-permute-start(bf16[2,192,1024]{2,1,0:T(8,128)(2,1)S(1)} %collective-permute-done.20.refs_14_), channel_id=1, source_target_pairs={{0,2},{1,3},{2,4},{3,5},{4,6},{5,7},{6,0},{7,1},{8,10},{9,11},{10,... | collective-permute-start | bytes 2359304 | tf_op jit(solution)/shard_map/ppermute | solution.py:223
  305.0 29.0 %collective-permute-start.19 = (bf16[2,192,1024]{2,1,0:T(8,128)(2,1)S(1)}, bf16[2,192,1024]{2,1,0:T(8,128)(2,1)S(1)}, u32[]{:S(2)}, u32[]{:S(2)}) collective-permute-start(bf16[2,192,1024]{2,1,0:T(8,128)(2,1)S(1)} %collective-permute-done.18.refs_12_), channel_id=1, source_target_pairs={{0,1},{1,0},{2,3},{3,2},{4,5},{5,4},{6,7},{7,6},{8,9},{9,8},{10,11... | collective-permute-start | bytes 2359304 | tf_op jit(solution)/shard_map/ppermute | solution.py:223
  305.1 28.9 %collective-permute-start.14 = (bf16[2,192,1024]{2,1,0:T(8,128)(2,1)S(1)}, bf16[2,192,1024]{2,1,0:T(8,128)(2,1)S(1)}, u32[]{:S(2)}, u32[]{:S(2)}) collective-permute-start(bf16[2,192,1024]{2,1,0:T(8,128)(2,1)S(1)} %collective-permute-done.13.refs_6_), channel_id=1, source_target_pairs={{0,1},{1,0},{2,3},{3,2},{4,5},{5,4},{6,7},{7,6},{8,9},{9,8},{10,11... | collective-permute-start | bytes 2359304 | tf_op jit(solution)/shard_map/ppermute | solution.py:223
  305.7 28.4 %collective-permute-start.21 = (bf16[2,192,1024]{2,1,0:T(8,128)(2,1)S(1)}, bf16[2,192,1024]{2,1,0:T(8,128)(2,1)S(1)}, u32[]{:S(2)}, u32[]{:S(2)}) collective-permute-start(bf16[2,192,1024]{2,1,0:T(8,128)(2,1)S(1)} %collective-permute-done.20.refs_14_), channel_id=1, source_target_pairs={{0,1},{1,0},{2,3},{3,2},{4,5},{5,4},{6,7},{7,6},{8,9},{9,8},{10,11... | collective-permute-start | bytes 2359304 | tf_op jit(solution)/shard_map/ppermute | solution.py:223
  (59 other events, 2425.6 us)
Sparse Core Ops, SparseCore 0:
  9.2 91.2 all-gather.6
  102.2 38.2 all-gather.4

commit v2 on v1

v2 whole, which is shorter than its diff:
```python
import functools

import jax
import jax.numpy as jnp
from jax import lax
from jax.experimental import pallas as pl
from jax.experimental.pallas import tpu as pltpu
from jax.sharding import PartitionSpec as P

NB = 32
HIGH = lax.Precision.HIGHEST
NN = (((1,), (0,)), ((), ()))
NT = (((1,), (1,)), ((), ()))
TN = (((0,), (0,)), ((), ()))


def mm(a, b, dims, precision=None):
    return lax.dot_general(a, b, dims, precision=precision, preferred_element_type=jnp.float32)


def invert_diagonal(blocks):
    nb = blocks[0].shape[0]
    row = lax.broadcasted_iota(jnp.int32, (nb, 2 * nb), 0)
    lane = lax.broadcasted_iota(jnp.int32, (nb, 2 * nb), 1)
    eye = (lane == row + nb).astype(jnp.float32)
    work = [jnp.concatenate([b, eye[:, nb:]], axis=1) for b in blocks]
    for j in range(nb - 1):
        for n, a in enumerate(work):
            pivot_row = a[j : j + 1, :]
            scaled = pivot_row / a[j : j + 1, j : j + 1]
            work[n] = a - jnp.where(row > j, a[:, j : j + 1], 0.0) * scaled
    out = []
    for a in work:
        d = jnp.sum(jnp.where(lane == row, a, 0.0), axis=1, keepdims=True)
        r = lax.rsqrt(d)
        r = r * (1.5 - 0.5 * d * r * r)
        out.append(a[:, nb:] * r)
    return out


def invert_cholesky(z_ref, n, width):
    for j in range(width // NB):
        lo, hi = j * NB, (j + 1) * NB
        inverses = invert_diagonal([z_ref[t, lo:hi, lo:hi] for t in range(n)])
        for t in range(n):
            panel = mm(inverses[t], z_ref[t, lo:hi, :], NN, HIGH)
            z_ref[t, lo:hi, :] = panel
            if hi < width:
                z_ref[t, hi:, :] = z_ref[t, hi:, :] - mm(panel[:, hi:width], panel, TN, HIGH)


def factor_kernel(n_col, n_row, chunk, *refs):
    place, help_l, rank_l, help_u, rank_u = refs[:5]
    tile_l, raw_u, sk_col = refs[5:8]
    sk_row = refs[8 : 8 + n_row]
    got_u = refs[8 + n_row : 7 + 2 * n_row]
    q_l, q_u, omega, tile, sketched, z, sem, sem_s = refs[7 + 2 * n_row :]
    my_row, my_col = place[0], place[1]
    n, width, order = sketched.shape
    slab = order // n_row

    copies = []
    for t in range(n):
        if t == 0:
            k = chunk * n_col + my_col
            mine = [
                pltpu.make_async_copy(sk_col.at[help_l[k]], omega.at[t], sem_s.at[t]),
                pltpu.make_async_copy(tile_l, tile.at[t], sem.at[t, 0]),
            ]
        else:
            k = chunk * n_col + (t - 1) * n_row + my_row
            mine = [pltpu.make_async_copy(sk_row[0], omega.at[t], sem_s.at[t])]
            away = jnp.bitwise_xor(my_row, help_u[k])
            for o in range(n_row):

                @pl.when(away == o)
                def _(o=o, t=t):
                    pltpu.make_async_copy(sk_row[o], omega.at[t], sem_s.at[t]).start()
            for d in range(n_row):
                j = jnp.bitwise_xor(my_row, d)
                src = raw_u.at[k] if d == 0 else got_u[d - 1].at[t - 1]
                dst = tile.at[t, pl.ds(pl.multiple_of(j * slab, slab), slab)]
                mine.append(pltpu.make_async_copy(src, dst, sem.at[t, d]))
        for c in mine[min(t, 1) :]:
            c.start()
        copies.append(mine)

    row = lax.broadcasted_iota(jnp.int32, (width, width), 0)
    lane = lax.broadcasted_iota(jnp.int32, (width, width), 1)
    eye = (row == lane).astype(jnp.float32)
    sub = lax.broadcasted_iota(jnp.int32, (width, order), 0)
    for t in range(n):
        for c in copies[t]:
            c.wait()
        if t == 0:
            q = rank_l[chunk * n_col + my_col]
        else:
            q = rank_u[chunk * n_col + (t - 1) * n_row + my_row]
        masked = jnp.where(sub < q, omega[t].astype(jnp.float32), 0.0).astype(jnp.bfloat16)
        sketched[t] = mm(masked, tile[t], NT)
        gram = mm(sketched[t], sketched[t], NT, HIGH) + jnp.where(row >= q, eye, 0.0)
        z[t] = jnp.concatenate([gram, eye], axis=1)
    invert_cholesky(z, n, width)
    for t in range(n):
        out = q_l if t == 0 else q_u.at[t - 1]
        basis = mm(z[t, :, width:], sketched[t], NN, HIGH).astype(jnp.bfloat16)
        out[0] = basis
        out[1] = mm(basis, tile[t], NN).astype(jnp.bfloat16)


def factor(chunk, place, help_l, rank_l, help_u, rank_u, tile_l, raw_u, sk_col, sk_row, got_u):
    n_col, n_row = sk_col.shape[0], len(sk_row)
    per = n_col // n_row
    n = 1 + per
    width, order = sk_col.shape[1:]
    smem = pl.BlockSpec(memory_space=pltpu.SMEM)
    hbm = pl.BlockSpec(memory_space=pl.ANY)
    vmem = pl.BlockSpec(memory_space=pltpu.VMEM)
    return pl.pallas_call(
        functools.partial(factor_kernel, n_col, n_row, chunk),
        out_shape=(
            jax.ShapeDtypeStruct((2, width, order), jnp.bfloat16),
            jax.ShapeDtypeStruct((per, 2, width, order), jnp.bfloat16),
        ),
        in_specs=[smem] * 5 + [hbm] * (2 + 2 * n_row),
        out_specs=(vmem, vmem),
        scratch_shapes=[
            pltpu.VMEM((n, width, order), jnp.bfloat16),
            pltpu.VMEM((n, order, order), jnp.bfloat16),
            pltpu.VMEM((n, width, order), jnp.float32),
            pltpu.VMEM((n, width, 2 * width), jnp.float32),
            pltpu.SemaphoreType.DMA((n, n_row)),
            pltpu.SemaphoreType.DMA((n,)),
        ],
        compiler_params=pltpu.CompilerParams(vmem_limit_bytes=56 * 2**20),
        cost_estimate=pl.CostEstimate(flops=35 * 10**9, bytes_accessed=12 * 2**20, transcendentals=0),
        name="factor_tiles",
    )(place, help_l, rank_l, help_u, rank_u, tile_l, raw_u, sk_col, *sk_row, *got_u)


def update_kernel(n_col, n_row, group, *refs):
    place, start, full_l = refs[:3]
    parts = refs[3 : 3 + n_col]
    out, ql, wl, qu, wu, left, sem, sem_t, tr = refs[3 + n_col :]
    my_row = place[0]
    width = ql.shape[1]
    load = pltpu.make_async_copy(start, tr, sem_t)
    load.start()
    for t in range(n_col // n_row):
        for o in range(n_row):
            k = t * n_row + jnp.bitwise_xor(my_row, o)
            src = parts[t * n_row + o]
            pltpu.make_async_copy(src.at[0], qu.at[k], sem.at[2, k]).start()
            pltpu.make_async_copy(src.at[1], wu.at[k], sem.at[3, k]).start()
        for o in range(n_row):
            k = t * n_row + o
            pltpu.make_async_copy(full_l.at[k, 1], wl.at[k], sem.at[1, k]).start()
            pltpu.make_async_copy(full_l.at[k, 0], ql.at[k], sem.at[0, k]).start()
    load.wait()
    out[...] = tr[...].astype(jnp.float32)

    def one_group(g, carry):
        for e in range(group):
            k = g * group + e
            for a, buf in enumerate((ql, wl, qu, wu)):
                pltpu.make_async_copy(buf.at[k], buf.at[k], sem.at[a, k]).wait()
            mid = mm(qu[k], wl[k], NT).astype(jnp.bfloat16)
            left[e * width : (e + 1) * width, :] = mm(mid, ql[k], NN).astype(jnp.bfloat16)
        coeff = wu[pl.ds(g * group, group)].reshape(group * width, wu.shape[2])
        out[...] = out[...] - mm(left[...], coeff, TN)
        return carry

    lax.fori_loop(0, n_col // group, one_group, 0)


def update(place, start, full_l, parts):
    n_col, n_row = full_l.shape[0], len(parts[0])
    width, order = full_l.shape[2:]
    group = 4
    smem = pl.BlockSpec(memory_space=pltpu.SMEM)
    hbm = pl.BlockSpec(memory_space=pl.ANY)
    vmem = pl.BlockSpec(memory_space=pltpu.VMEM)
    held = pltpu.VMEM((n_col, width, order), jnp.bfloat16)
    return pl.pallas_call(
        functools.partial(update_kernel, n_col, n_row, group),
        out_shape=jax.ShapeDtypeStruct(start.shape, jnp.float32),
        in_specs=[smem] + [hbm] * (2 + n_col),
        out_specs=vmem,
        scratch_shapes=[held, held, held, held]
        + [
            pltpu.VMEM((group * width, order), jnp.bfloat16),
            pltpu.SemaphoreType.DMA((4, n_col)),
            pltpu.SemaphoreType.DMA,
            pltpu.VMEM(start.shape, start.dtype),
        ],
        compiler_params=pltpu.CompilerParams(vmem_limit_bytes=56 * 2**20),
        cost_estimate=pl.CostEstimate(flops=15 * 10**9, bytes_accessed=20 * 2**20, transcendentals=0),
        name="update_tile",
    )(place, start, full_l, *parts[0], *parts[1])


def shift(x, axis, size, move):
    return lax.ppermute(x, axis, [(i, move(i)) for i in range(size)])


def exchange_u(raw, n_row):
    me = lax.axis_index("row")
    x = raw.reshape((-1, n_row) + raw.shape[1:])
    return [
        shift(
            lax.dynamic_index_in_dim(x, jnp.bitwise_xor(me, d), 1, False),
            "row",
            n_row,
            lambda i: i ^ d,
        )
        for d in range(1, n_row)
    ]


def spread_row(x, n_row):
    return [x] + [shift(x, "row", n_row, lambda i: i ^ o) for o in range(1, n_row)]


def gather_row_first(pieces, n_row):
    bits = [1 << b for b in range(n_row.bit_length() - 1)]
    out = []
    for number, piece in enumerate(pieces):
        turn = number % len(bits)
        order = bits[turn:] + bits[:turn]
        b = order[0]
        out.append((order[1:], {0: piece, b: shift(piece, "row", n_row, lambda i: i ^ b)}))
    return out


def gather_row_rest(begun, n_row):
    out = []
    for order, held in begun:
        held = dict(held)
        for b in order:
            held.update({o ^ b: shift(p, "row", n_row, lambda i: i ^ b) for o, p in held.items()})
        out.append([held[o] for o in range(n_row)])
    return out


def local(trailing, raw_l, raw_u, sketch, helper_l, helper_u, ranks_l, ranks_u):
    n_col, n_row = lax.axis_size("col"), lax.axis_size("row")
    place = jnp.stack([lax.axis_index("row"), lax.axis_index("col")]).astype(jnp.int32)
    mine_l, mine_u = raw_l[0], raw_u[:, 0]
    chunks = mine_l.shape[0] // n_col
    per = n_col // n_row
    own = jnp.swapaxes(sketch[0, 0], 0, 1)
    sk_col = lax.all_gather(own[None], "col", axis=0, tiled=True)
    sk_row = spread_row(own, n_row)

    def exchange(c, raw):
        part = slice(c * n_col, (c + 1) * n_col)
        tile_l = lax.all_to_all(raw[0][part], "col", 0, 0, tiled=True)
        return tile_l.reshape(-1, tile_l.shape[2]), exchange_u(raw[1][part], n_row)

    def make(c, got):
        return factor(
            c, place, helper_l[0], ranks_l[0], helper_u[:, 0], ranks_u[:, 0],
            got[0], mine_u, sk_col, sk_row, got[1],
        )

    def gather(made, begun):
        full_l = lax.all_gather(made[0][None], "col", axis=0, tiled=True)
        return full_l, gather_row_rest(begun, n_row)

    def begin(made):
        return gather_row_first([made[1][t] for t in range(per)], n_row)

    got = exchange(0, (mine_l, mine_u))
    made = None
    result = trailing
    for c in range(chunks):
        sk_row, later = lax.optimization_barrier((sk_row, (mine_l, mine_u)))
        coming = exchange(c + 1, later) if c + 1 < chunks else None
        if made is not None:
            begun = begin(made)
            held = [h for _, h in begun]
            got, held = lax.optimization_barrier((got, held))
            gathered = gather(made, [(o, h) for (o, _), h in zip(begun, held)])
        fresh = make(c, got)
        if made is not None:
            gathered, fresh = lax.optimization_barrier((gathered, fresh))
            result = update(place, result, *gathered)
        elif coming is not None:
            coming, fresh = lax.optimization_barrier((coming, fresh))
        made, got = fresh, coming
    gathered = gather(made, begin(made))
    return update(place, result, *gathered)


def solution(mesh):
    placed = (
        P("row", "col"),
        P("row", None, "col", None),
        P(None, "col", "row", None),
        P("row", "col", None, None),
        P("row", None),
        P(None, "col"),
        P("row", None),
        P(None, "col"),
    )
    return jax.shard_map(
        local, mesh=mesh, in_specs=placed, out_specs=P("row", "col"), check_vma=False
    )
```

time: 375 us -> 311 us (0.83)
  waiting for transfers between devices: 240 us -> 135 us
  Pallas kernels: 77.8 us -> 100 us
  local copies, waits for them, and re-layouts: 12.4 us -> 24.9 us
  starting transfers between devices: 27.9 us -> 34.8 us
    ppermute x36 -> x21, waiting for transfers between devices: 222 us -> 121 us  [shift(): return lax.ppermute(x, axis, [(i, move(i)) for i in range(size)])]
    pallas_call x2 -> x4, Pallas kernels: 77.8 us -> 100 us  [the longest x2 65.5 us: factor(): pl.pallas_call(functools.partial(factor_kernel, n_col, n_row, chunk), out...]
    all_to_all x0 -> x2, starting transfers between devices: none -> 11.1 us  [exchange(): tile_l = lax.all_to_all(raw[0][part], 'col', 0, 0, tiled=True)]
    slice x2 -> x4, local copies, waits for them, and re-layouts: 2.33 us -> 12.4 us  [the longest x2 7.65 us: exchange(): raw[1][part]]
    ppermute x36 -> x21, starting transfers between devices: 27.8 us -> 23.5 us  [shift(): return lax.ppermute(x, axis, [(i, move(i)) for i in range(size)])]
    all_gather x2 -> x3, waiting for transfers between devices: 16.8 us -> 12.6 us  [the longest x2 12.6 us: gather(): full_l = lax.all_gather(made[0][None], 'col', axis=0, tiled=True)]
  transfers between devices with their start and end apart: 38 -> 26, of which waited for: 21 -> 8; matrix products, arithmetic and copies ran while one was open for 2% -> 7% of each run, Pallas kernels for 0% -> 27%
where the time goes in v2:
time: 311 us; the launch traced here: 309 us
  waiting for transfers between devices  135 us (43%)
  Pallas kernels  100 us (32%)
  starting transfers between devices  34.8 us (11%)
  local copies, waits for them, and re-layouts  24.9 us (8%)
  between operations  13.6 us (4%)
    ppermute x21, waiting for transfers between devices, shift(): return lax.ppermute(x, axis, [(i, move(i)) for i in range(size)])  121 us
    pallas_call x2, Pallas kernels, factor(): pl.pallas_call(functools.partial(factor_kernel, n_col, n_row, chunk), out...  65.5 us
    pallas_call x2, Pallas kernels, update(): pl.pallas_call(functools.partial(update_kernel, n_col, n_row, group), out...  34.6 us
    ppermute x21, starting transfers between devices, shift(): return lax.ppermute(x, axis, [(i, move(i)) for i in range(size)])  23.5 us
    all_gather x2, waiting for transfers between devices, gather(): full_l = lax.all_gather(made[0][None], 'col', axis=0, tiled=True)  12.6 us
    all_to_all x2, starting transfers between devices, exchange(): tile_l = lax.all_to_all(raw[0][part], 'col', 0, 0, tiled=True)  11.1 us
    slice x2, local copies, waits for them, and re-layouts, exchange(): raw[1][part]  7.65 us
  transfers between devices with their start and end apart: 26, of which 8 were waited for; matrix products, arithmetic and copies ran while one was open for 7% of the time, Pallas kernels for 27%

profile of v2, /device:TPU:0, one launch (start us, length us, event | category | flops | bytes accessed | tf_op | source)
XLA Modules:
  0.0 308.6 jit_solution(1088459182689212700)
XLA Ops:
  7.3 3.2 %slice_bitcast_fusion = bf16[8,128,1024]{2,1,0:T(8,128)(2,1)} fusion(bf16[1,16,128,1024]{3,2,1,0:T(8,128)(2,1)} %param.9), kind=kLoop, calls=%fused_computation | loop fusion | bytes 4194304 | tf_op jit(solution)/shard_map/slice | solution.py:257
  10.4 6.3 %all-to-all-start.1 = ((bf16[8,128,1024]{2,1,0:T(8,128)(2,1)}), bf16[8,128,1024]{2,1,0:T(8,128)(2,1)S(1)}, u32[]{:S(2)}, u32[]{:S(2)}) async-start(bf16[8,128,1024]{2,1,0:T(8,128)(2,1)} %slice_bitcast_fusion), calls=%async_computation.1 | async-start | bytes 4194304 | tf_op jit(solution)/shard_map/all_to_all | solution.py:257
  16.8 1.6 collective-permute-start
  18.3 5.0 %slice.32 = bf16[8,1,256,1024]{3,2,1,0:T(8,128)(2,1)} slice(bf16[16,1,256,1024]{3,2,1,0:T(8,128)(2,1)} %param.10), slice={[0:8], [0:1], [0:256], [0:1024]} | slice | bytes 8388608 | tf_op jit(solution)/shard_map/slice | solution.py:258
  23.4 3.8 %dynamic-slice_bitcast_fusion = (bf16[2,256,1024]{2,1,0:T(8,128)(2,1)S(1)}, bf16[2,256,1024]{2,1,0:T(8,128)(2,1)}, bf16[2,256,1024]{2,1,0:T(8,128)(2,1)}) fusion(bf16[2,4,256,1024]{3,2,1,0:T(8,128)(2,1)} %bitcast.52, s32[]{:T(128)S(6)} %select_n.15, s32[]{:T(128)S(6)} %select_n.14, s32[]{:T(128)S(6)} %select_n.13), kind=kLoop, calls=%fused_computation.1 | loop fusion | bytes 6291468 | tf_op jit(solution)/shard_map/jit(dynamic_index_in_dim)/squeeze | solution.py:211
  29.1 1.6 collective-permute-start.8
  32.5 59.5 %collective-permute-done.1.refs_10_ = bf16[192,1024]{1,0:T(8,128)(2,1)S(1)} collective-permute-done((bf16[192,1024]{1,0:T(8,128)(2,1)S(1)}, bf16[192,1024]{1,0:T(8,128)(2,1)S(1)}, u32[]{:S(2)}, u32[]{:S(2)}) %collective-permute-start.1) | collective-permute-done | bytes 393248 | tf_op jit(solution)/shard_map/ppermute | solution.py:203
  93.5 1.5 slice.28
  95.1 4.8 %all-to-all-start = ((bf16[8,128,1024]{2,1,0:T(8,128)(2,1)}), bf16[8,128,1024]{2,1,0:T(8,128)(2,1)}, u32[]{:S(2)}, u32[]{:S(2)}) async-start(bf16[8,128,1024]{2,1,0:T(8,128)(2,1)} %slice.28), calls=%async_computation | async-start | bytes 4194304 | tf_op jit(solution)/shard_map/all_to_all | solution.py:257
  100.7 2.6 slice.29
  104.6 1.6 collective-permute-start.3
  106.2 1.6 collective-permute-start.4
  108.1 32.9 %factor_tiles.2 = (bf16[2,192,1024]{2,1,0:T(8,128)(2,1)}, bf16[2,2,192,1024]{3,2,1,0:T(8,128)(2,1)}) custom-call(s32[2]{0:T(128)} %pad_add_fusion.refs_0_, s32[16]{0:T(128)} %bitcast.69, s32[16]{0:T(128)} %bitcast.71, s32[16]{0:T(128)} %bitcast.73, s32[16]{0:T(128)} %bitcast.75, bf16[1024,1024]{1,0:T(8,128)(2,1)} %bitcast.58, ...), custom_call_target="tpu_custom_call" | custom-call | flops 35000000512 | bytes 12582912 | tf_op jit(solution)/shard_map/factor_tiles/pallas_call | solution.py:119
  141.0 13.0 %collective-permute-done.4.refs_13_ = bf16[2,256,1024]{2,1,0:T(8,128)(2,1)} collective-permute-done((bf16[2,256,1024]{2,1,0:T(8,128)(2,1)S(1)}, bf16[2,256,1024]{2,1,0:T(8,128)(2,1)}, u32[]{:S(2)}, u32[]{:S(2)}) %collective-permute-start.4) | collective-permute-done | bytes 1048608 | tf_op jit(solution)/shard_map/ppermute | solution.py:203
  155.6 1.6 collective-permute-start.10
  157.6 17.1 %collective-permute-done.10.refs_9_ = bf16[2,192,1024]{2,1,0:T(8,128)(2,1)S(1)} collective-permute-done((bf16[2,192,1024]{2,1,0:T(8,128)(2,1)S(1)}, bf16[2,192,1024]{2,1,0:T(8,128)(2,1)S(1)}, u32[]{:S(2)}, u32[]{:S(2)}) %collective-permute-start.10) | collective-permute-done | bytes 786464 | tf_op jit(solution)/shard_map/ppermute | solution.py:203
  179.8 32.6 %factor_tiles.3 = (bf16[2,192,1024]{2,1,0:T(8,128)(2,1)}, bf16[2,2,192,1024]{3,2,1,0:T(8,128)(2,1)}) custom-call(s32[2]{0:T(128)} %pad_add_fusion.refs_0_, s32[16]{0:T(128)} %bitcast.70, s32[16]{0:T(128)} %bitcast.72, s32[16]{0:T(128)} %bitcast.74, s32[16]{0:T(128)} %bitcast.76, bf16[1024,1024]{1,0:T(8,128)(2,1)} %bitcast.7.refs_5_, ...), custom_call_target="tpu_custom_call" | custom-call | flops 35000000512 | bytes 12582912 | tf_op jit(solution)/shard_map/factor_tiles/pallas_call | solution.py:119
  214.5 4.6 %all-gather.9.cloned.1.call-done = bf16[16,192,1024]{2,1,0:T(8,128)(2,1)} async-done(((bf16[2,192,1024]{2,1,0:T(8,128)(2,1)}), bf16[16,192,1024]{2,1,0:T(8,128)(2,1)}) %all-gather.9.cloned.1.call-update) | async-done | bytes 6291472 | tf_op jit(solution)/shard_map/all_gather | solution.py:267
  220.7 1.5 collective-permute-start.15
  224.8 16.3 %collective-permute-done.15.refs_4_ = bf16[2,192,1024]{2,1,0:T(8,128)(2,1)S(1)} collective-permute-done((bf16[2,192,1024]{2,1,0:T(8,128)(2,1)S(1)}, bf16[2,192,1024]{2,1,0:T(8,128)(2,1)S(1)}, u32[]{:S(2)}, u32[]{:S(2)}) %collective-permute-start.15) | collective-permute-done | bytes 786464 | tf_op jit(solution)/shard_map/ppermute | solution.py:203
  244.1 17.0 %update_tile.2.refs_1_ = f32[1024,1024]{1,0:T(8,128)} custom-call(s32[2]{0:T(128)} %pad_add_fusion.refs_0_, bf16[1024,1024]{1,0:T(8,128)(2,1)} %refs_1_.1, bf16[8,2,192,1024]{3,2,1,0:T(8,128)(2,1)} %bitcast.65, bf16[2,192,1024]{2,1,0:T(8,128)(2,1)} %copy-done.3, bf16[2,192,1024]{2,1,0:T(8,128)(2,1)} %copy-done.8, bf16[2,192,1024]{2,1,0:T(8,128)(2,1)} %copy-done.9, ...), custom_call_target="tpu_custom_call" | custom-call | flops 15000000512 | bytes 20971520 | tf_op jit(solution)/shard_map/update_tile/pallas_call | solution.py:184
  261.2 14.2 %collective-permute-done.17.refs_6_ = bf16[2,192,1024]{2,1,0:T(8,128)(2,1)S(1)} collective-permute-done((bf16[2,192,1024]{2,1,0:T(8,128)(2,1)S(1)}, bf16[2,192,1024]{2,1,0:T(8,128)(2,1)S(1)}, u32[]{:S(2)}, u32[]{:S(2)}) %collective-permute-start.17) | collective-permute-done | bytes 786464 | tf_op jit(solution)/shard_map/ppermute | solution.py:203
  276.3 8.0 %all-gather.11.cloned.1.call-done = bf16[16,192,1024]{2,1,0:T(8,128)(2,1)} async-done(((bf16[2,192,1024]{2,1,0:T(8,128)(2,1)}), bf16[16,192,1024]{2,1,0:T(8,128)(2,1)}) %all-gather.11.cloned.1.call-update) | async-done | bytes 6291472 | tf_op jit(solution)/shard_map/all_gather | solution.py:267
  284.3 17.6 %update_tile.3 = f32[1024,1024]{1,0:T(8,128)} custom-call(s32[2]{0:T(128)} %pad_add_fusion.refs_0_, f32[1024,1024]{1,0:T(8,128)} %update_tile.2.refs_1_, bf16[8,2,192,1024]{3,2,1,0:T(8,128)(2,1)} %bitcast.66, bf16[2,192,1024]{2,1,0:T(8,128)(2,1)} %copy-done.5, bf16[2,192,1024]{2,1,0:T(8,128)(2,1)} %copy-done.12, bf16[2,192,1024]{2,1,0:T(8,128)(2,1)} %copy-done.14, ...), custom_call_target="tpu_custom_call" | custom-call | flops 15000000512 | bytes 20971520 | tf_op jit(solution)/shard_map/update_tile/pallas_call | solution.py:184
  (82 shorter events, 25.5 us)
Async XLA Ops:
  6.5 101.6 %all-gather.7.cloned.1.call-start = ((), (), s32[]{:S(2)}) async-start(), calls=%async_computation.2 | async-start | bytes 3538944 | tf_op jit(solution)/shard_map/all_gather | solution.py:252
  10.4 84.6 %all-to-all-start.1 = ((bf16[8,128,1024]{2,1,0:T(8,128)(2,1)}), bf16[8,128,1024]{2,1,0:T(8,128)(2,1)S(1)}, u32[]{:S(2)}, u32[]{:S(2)}) async-start(bf16[8,128,1024]{2,1,0:T(8,128)(2,1)} %slice_bitcast_fusion), calls=%async_computation.1 | async-start | bytes 4194304 | tf_op jit(solution)/shard_map/all_to_all | solution.py:257
  27.2 80.5 %collective-permute-start.6 = (bf16[2,256,1024]{2,1,0:T(8,128)(2,1)}, bf16[2,256,1024]{2,1,0:T(8,128)(2,1)}, u32[]{:S(2)}, u32[]{:S(2)}) collective-permute-start(bf16[2,256,1024]{2,1,0:T(8,128)(2,1)} %get-tuple-element.85), channel_id=1, source_target_pairs={{0,8},{8,0},{16,24},{24,16},{1,9},{9,1},{17,25},{25,17},{2,10},{10... | collective-permute-start | bytes 3145736 | tf_op jit(solution)/shard_map/ppermute | solution.py:203
  27.5 80.6 %collective-permute-start.7 = (bf16[2,256,1024]{2,1,0:T(8,128)(2,1)}, bf16[2,256,1024]{2,1,0:T(8,128)(2,1)}, u32[]{:S(2)}, u32[]{:S(2)}) collective-permute-start(bf16[2,256,1024]{2,1,0:T(8,128)(2,1)} %get-tuple-element.84), channel_id=1, source_target_pairs={{0,16},{8,24},{16,0},{24,8},{1,17},{9,25},{17,1},{25,9},{2,18},{10... | collective-permute-start | bytes 3145736 | tf_op jit(solution)/shard_map/ppermute | solution.py:203
  29.1 79.0 %collective-permute-start.8 = (bf16[2,256,1024]{2,1,0:T(8,128)(2,1)S(1)}, bf16[2,256,1024]{2,1,0:T(8,128)(2,1)}, u32[]{:S(2)}, u32[]{:S(2)}) collective-permute-start(bf16[2,256,1024]{2,1,0:T(8,128)(2,1)S(1)} %get-tuple-element.83), channel_id=1, source_target_pairs={{0,24},{8,16},{16,8},{24,0},{1,25},{9,17},{17,9},{25,1},{2,26},{10... | collective-permute-start | bytes 3145736 | tf_op jit(solution)/shard_map/ppermute | solution.py:203
  30.7 61.3 %collective-permute-start.1 = (bf16[192,1024]{1,0:T(8,128)(2,1)S(1)}, bf16[192,1024]{1,0:T(8,128)(2,1)S(1)}, u32[]{:S(2)}, u32[]{:S(2)}) collective-permute-start(bf16[192,1024]{1,0:T(8,128)(2,1)S(1)} %bitcast.63), channel_id=1, source_target_pairs={{0,16},{8,24},{16,0},{24,8},{1,17},{9,25},{17,1},{25,9},{2,18},{10... | collective-permute-start | bytes 1179656 | tf_op jit(solution)/shard_map/ppermute | solution.py:203
  32.1 59.9 %collective-permute-start.2 = (bf16[192,1024]{1,0:T(8,128)(2,1)S(1)}, bf16[192,1024]{1,0:T(8,128)(2,1)S(1)}, u32[]{:S(2)}, u32[]{:S(2)}) collective-permute-start(bf16[192,1024]{1,0:T(8,128)(2,1)S(1)} %bitcast.64), channel_id=1, source_target_pairs={{0,24},{8,16},{16,8},{24,0},{1,25},{9,17},{17,9},{25,1},{2,26},{10... | collective-permute-start | bytes 1179656 | tf_op jit(solution)/shard_map/ppermute | solution.py:203
  95.1 59.0 %all-to-all-start = ((bf16[8,128,1024]{2,1,0:T(8,128)(2,1)}), bf16[8,128,1024]{2,1,0:T(8,128)(2,1)}, u32[]{:S(2)}, u32[]{:S(2)}) async-start(bf16[8,128,1024]{2,1,0:T(8,128)(2,1)} %slice.28), calls=%async_computation | async-start | bytes 4194304 | tf_op jit(solution)/shard_map/all_to_all | solution.py:257
  99.8 119.3 %all-gather.9.cloned.1.call-start = ((), (), s32[]{:S(2)}) async-start(), calls=%async_computation.3 | async-start | bytes 7077888 | tf_op jit(solution)/shard_map/all_gather | solution.py:267
  104.6 36.4 %collective-permute-start.3 = (bf16[2,256,1024]{2,1,0:T(8,128)(2,1)}, bf16[2,256,1024]{2,1,0:T(8,128)(2,1)}, u32[]{:S(2)}, u32[]{:S(2)}) collective-permute-start(bf16[2,256,1024]{2,1,0:T(8,128)(2,1)} %get-tuple-element.88), channel_id=1, source_target_pairs={{0,8},{8,0},{16,24},{24,16},{1,9},{9,1},{17,25},{25,17},{2,10},{10... | collective-permute-start | bytes 3145736 | tf_op jit(solution)/shard_map/ppermute | solution.py:203
  106.2 47.8 %collective-permute-start.4 = (bf16[2,256,1024]{2,1,0:T(8,128)(2,1)S(1)}, bf16[2,256,1024]{2,1,0:T(8,128)(2,1)}, u32[]{:S(2)}, u32[]{:S(2)}) collective-permute-start(bf16[2,256,1024]{2,1,0:T(8,128)(2,1)S(1)} %get-tuple-element.87), channel_id=1, source_target_pairs={{0,16},{8,24},{16,0},{24,8},{1,17},{9,25},{17,1},{25,9},{2,18},{10... | collective-permute-start | bytes 3145736 | tf_op jit(solution)/shard_map/ppermute | solution.py:203
  107.7 46.3 %collective-permute-start.5 = (bf16[2,256,1024]{2,1,0:T(8,128)(2,1)S(1)}, bf16[2,256,1024]{2,1,0:T(8,128)(2,1)}, u32[]{:S(2)}, u32[]{:S(2)}) collective-permute-start(bf16[2,256,1024]{2,1,0:T(8,128)(2,1)S(1)} %get-tuple-element.86), channel_id=1, source_target_pairs={{0,24},{8,16},{16,8},{24,0},{1,25},{9,17},{17,9},{25,1},{2,26},{10... | collective-permute-start | bytes 3145736 | tf_op jit(solution)/shard_map/ppermute | solution.py:203
  154.1 130.2 %all-gather.11.cloned.1.call-start = ((), (), s32[]{:S(2)}) async-start(), calls=%async_computation.4 | async-start | bytes 7077888 | tf_op jit(solution)/shard_map/all_gather | solution.py:267
  155.6 19.1 %collective-permute-start.10 = (bf16[2,192,1024]{2,1,0:T(8,128)(2,1)S(1)}, bf16[2,192,1024]{2,1,0:T(8,128)(2,1)S(1)}, u32[]{:S(2)}, u32[]{:S(2)}) collective-permute-start(bf16[2,192,1024]{2,1,0:T(8,128)(2,1)S(1)} %get-tuple-element.77.refs_7_), channel_id=1, source_target_pairs={{0,16},{8,24},{16,0},{24,8},{1,17},{9,25},{17,1},{25,9},{2,18},{10... | collective-permute-start | bytes 2359304 | tf_op jit(solution)/shard_map/ppermute | solution.py:203
  175.8 36.7 %collective-permute-start.11 = (bf16[2,192,1024]{2,1,0:T(8,128)(2,1)S(1)}, bf16[2,192,1024]{2,1,0:T(8,128)(2,1)S(1)}, u32[]{:S(2)}, u32[]{:S(2)}) collective-permute-start(bf16[2,192,1024]{2,1,0:T(8,128)(2,1)S(1)} %get-tuple-element.73.refs_3_), channel_id=1, source_target_pairs={{0,16},{8,24},{16,0},{24,8},{1,17},{9,25},{17,1},{25,9},{2,18},{10... | collective-permute-start | bytes 2359304 | tf_op jit(solution)/shard_map/ppermute | solution.py:203
  176.5 36.1 %collective-permute-start.12 = (bf16[2,192,1024]{2,1,0:T(8,128)(2,1)S(1)}, bf16[2,192,1024]{2,1,0:T(8,128)(2,1)S(1)}, u32[]{:S(2)}, u32[]{:S(2)}) collective-permute-start(bf16[2,192,1024]{2,1,0:T(8,128)(2,1)S(1)} %collective-permute-done.9.refs_4_), channel_id=1, source_target_pairs={{0,16},{8,24},{16,0},{24,8},{1,17},{9,25},{17,1},{25,9},{2,18},{10... | collective-permute-start | bytes 2359304 | tf_op jit(solution)/shard_map/ppermute | solution.py:203
  177.8 34.8 %collective-permute-start.13 = (bf16[2,192,1024]{2,1,0:T(8,128)(2,1)S(1)}, bf16[2,192,1024]{2,1,0:T(8,128)(2,1)S(1)}, u32[]{:S(2)}, u32[]{:S(2)}) collective-permute-start(bf16[2,192,1024]{2,1,0:T(8,128)(2,1)S(1)} %get-tuple-element.77.refs_7_), channel_id=1, source_target_pairs={{0,8},{8,0},{16,24},{24,16},{1,9},{9,1},{17,25},{25,17},{2,10},{10... | collective-permute-start | bytes 2359304 | tf_op jit(solution)/shard_map/ppermute | solution.py:203
  178.5 36.0 %collective-permute-start.14 = (bf16[2,192,1024]{2,1,0:T(8,128)(2,1)S(1)}, bf16[2,192,1024]{2,1,0:T(8,128)(2,1)}, u32[]{:S(2)}, u32[]{:S(2)}) collective-permute-start(bf16[2,192,1024]{2,1,0:T(8,128)(2,1)S(1)} %collective-permute-done.10.refs_9_), channel_id=1, source_target_pairs={{0,8},{8,0},{16,24},{24,16},{1,9},{9,1},{17,25},{25,17},{2,10},{10... | collective-permute-start | bytes 2359304 | tf_op jit(solution)/shard_map/ppermute | solution.py:203
  220.7 20.4 %collective-permute-start.15 = (bf16[2,192,1024]{2,1,0:T(8,128)(2,1)S(1)}, bf16[2,192,1024]{2,1,0:T(8,128)(2,1)S(1)}, u32[]{:S(2)}, u32[]{:S(2)}) collective-permute-start(bf16[2,192,1024]{2,1,0:T(8,128)(2,1)S(1)} %get-tuple-element.90.refs_3_), channel_id=1, source_target_pairs={{0,8},{8,0},{16,24},{24,16},{1,9},{9,1},{17,25},{25,17},{2,10},{10... | collective-permute-start | bytes 2359304 | tf_op jit(solution)/shard_map/ppermute | solution.py:203
  222.3 20.4 %collective-permute-start.19 = (bf16[2,192,1024]{2,1,0:T(8,128)(2,1)S(1)}, bf16[2,192,1024]{2,1,0:T(8,128)(2,1)S(1)}, u32[]{:S(2)}, u32[]{:S(2)}) collective-permute-start(bf16[2,192,1024]{2,1,0:T(8,128)(2,1)S(1)} %get-tuple-element.89.refs_7_), channel_id=1, source_target_pairs={{0,16},{8,24},{16,0},{24,8},{1,17},{9,25},{17,1},{25,9},{2,18},{10... | collective-permute-start | bytes 2359304 | tf_op jit(solution)/shard_map/ppermute | solution.py:203
  223.7 37.4 %collective-permute-start.16 = (bf16[2,192,1024]{2,1,0:T(8,128)(2,1)S(1)}, bf16[2,192,1024]{2,1,0:T(8,128)(2,1)S(1)}, u32[]{:S(2)}, u32[]{:S(2)}) collective-permute-start(bf16[2,192,1024]{2,1,0:T(8,128)(2,1)S(1)} %get-tuple-element.90.refs_3_), channel_id=1, source_target_pairs={{0,16},{8,24},{16,0},{24,8},{1,17},{9,25},{17,1},{25,9},{2,18},{10... | collective-permute-start | bytes 2359304 | tf_op jit(solution)/shard_map/ppermute | solution.py:203
  224.3 36.9 %collective-permute-start.18 = (bf16[2,192,1024]{2,1,0:T(8,128)(2,1)S(1)}, bf16[2,192,1024]{2,1,0:T(8,128)(2,1)S(1)}, u32[]{:S(2)}, u32[]{:S(2)}) collective-permute-start(bf16[2,192,1024]{2,1,0:T(8,128)(2,1)S(1)} %get-tuple-element.89.refs_7_), channel_id=1, source_target_pairs={{0,8},{8,0},{16,24},{24,16},{1,9},{9,1},{17,25},{25,17},{2,10},{10... | collective-permute-start | bytes 2359304 | tf_op jit(solution)/shard_map/ppermute | solution.py:203
  241.2 34.2 %collective-permute-start.17 = (bf16[2,192,1024]{2,1,0:T(8,128)(2,1)S(1)}, bf16[2,192,1024]{2,1,0:T(8,128)(2,1)S(1)}, u32[]{:S(2)}, u32[]{:S(2)}) collective-permute-start(bf16[2,192,1024]{2,1,0:T(8,128)(2,1)S(1)} %collective-permute-done.15.refs_4_), channel_id=1, source_target_pairs={{0,16},{8,24},{16,0},{24,8},{1,17},{9,25},{17,1},{25,9},{2,18},{10... | collective-permute-start | bytes 2359304 | tf_op jit(solution)/shard_map/ppermute | solution.py:203
  242.7 33.6 %collective-permute-start.20 = (bf16[2,192,1024]{2,1,0:T(8,128)(2,1)S(1)}, bf16[2,192,1024]{2,1,0:T(8,128)(2,1)}, u32[]{:S(2)}, u32[]{:S(2)}) collective-permute-start(bf16[2,192,1024]{2,1,0:T(8,128)(2,1)S(1)} %collective-permute-done.19.refs_9_), channel_id=1, source_target_pairs={{0,8},{8,0},{16,24},{24,16},{1,9},{9,1},{17,25},{25,17},{2,10},{10... | collective-permute-start | bytes 2359304 | tf_op jit(solution)/shard_map/ppermute | solution.py:203
  (21 other events, 463.0 us)
Sparse Core Ops, SparseCore 0:
  9.0 75.2 all-gather.6
  154.2 64.9 all-gather.8
  220.8 63.3 all-gather.10
